TPU v7x, 512 devices: a whole 4x8x8 slice. The times are simulated.
512 devices in a mesh: ctx: 32 (over x, z), batch: 16 (over y, core).
Axes of the slice: x: 4, y: 8, z: 8, core: 2. Of those that a mesh axis runs over, the one named last changes fastest.
Arguments:
- latent_cache: bfloat16 [32, 32768, 576], P('batch', 'ctx'), may hold values from -6 to 6
- queries: bfloat16 [8, 32, 128, 576], P(None, 'batch', 'ctx'), may hold values from -72 to 72
- new_latent: bfloat16 [8, 32, 576], P(None, 'batch'), may hold values from -9 to 9
- lengths: int32 [32], P('batch'), may hold values from 4096 to 32768, as said below
- selection: int32 [8, 32, 32], P(None, 'batch'), may hold values from 0 to 511, as said below
- w_uv: bfloat16 [128, 512, 128], P('ctx'), may hold values from -0.5 to 0.5
- w_out: bfloat16 [16384, 7168], P('ctx', 'batch'), may hold values from -0.1875 to 0.1875
Outputs:
- attention_out: bfloat16 [256, 7168], P('ctx', 'batch')
Inputs may be any that keep to these rules, and one draw needn't show every extreme that they name: `lengths`: every row holds at least 4096 positions; one row holds exactly that many and another exactly 32768. `selection`: for each step and row, 32 distinct block numbers in ascending order, each block starting below the row's length. At most 8 of them fall in one context shard (an aligned run of 16 blocks), and some row of every draw has exactly 8 in a shard.
All inputs are finite; a program needn't handle non-finite values.
Results may differ from a plain program's by a relative error of at most 0.022.
Values may be sent and summed in bfloat16 or wider, within the bound.
No kernel may reach another device: no remote copies, remote signals or barrier semaphores. Data moves between devices by JAX's collectives and lax.ppermute only.
A program may use at most 128 MiB of HBM per device.

v0:
```python
import jax
import jax.numpy as jnp
from jax import lax
from jax.sharding import PartitionSpec as P

BLOCK = 64


neg_fill = -1e30
score_scale = 192.0 ** (-0.5)


def local_partial(query_rows, latent_cache, chosen, lengths, shard_id, latent_width):
    rows_here, ctx_dev, width = latent_cache.shape
    positions = shard_id * ctx_dev + jnp.arange(ctx_dev, dtype=jnp.int32)
    live_mask = jnp.repeat(chosen, BLOCK, axis=1) & (positions[None, :] < lengths[:, None])
    scores = (
        jnp.einsum("rhd,rjd->rhj", query_rows, latent_cache, preferred_element_type=jnp.float32)
        * score_scale
    )
    masked = jnp.where(live_mask[:, None, :], scores, neg_fill)
    maxima = jnp.max(masked, axis=2).astype(jnp.bfloat16)
    weights = jnp.where(
        live_mask[:, None, :], jnp.exp(scores - maxima.astype(jnp.float32)[:, :, None]), 0.0
    )
    totals = jnp.sum(weights, axis=2).astype(jnp.bfloat16)
    summed = jnp.einsum(
        "rhj,rjl->rhl",
        weights.astype(jnp.bfloat16),
        latent_cache[:, :, :latent_width],
        preferred_element_type=jnp.float32,
    ).astype(jnp.bfloat16)
    return (summed, maxima, totals)


def body(latent_cache, queries, new_latent, lengths, selection, w_uv, w_out):
    steps_total = queries.shape[0]
    latent_width = w_uv.shape[1]
    shard_id = lax.axis_index("ctx")
    shard_blocks = latent_cache.shape[1] // BLOCK
    block_ids = shard_id * shard_blocks + jnp.arange(shard_blocks, dtype=jnp.int32)
    all_queries = lax.all_gather(queries, "ctx", axis=2, tiled=True)
    sum_list = []
    max_list = []
    total_list = []
    for step_index in range(steps_total):
        chosen = jnp.any(selection[step_index][:, :, None] == block_ids[None, None, :], axis=1)
        summed, maxima, totals = local_partial(
            all_queries[step_index], latent_cache, chosen, lengths, shard_id, latent_width
        )
        got_sums, got_maxima, got_totals = (
            lax.all_to_all(summed[None], "ctx", split_axis=2, concat_axis=0, tiled=True),
            lax.all_to_all(maxima[None], "ctx", split_axis=2, concat_axis=0, tiled=True),
            lax.all_to_all(totals[None], "ctx", split_axis=2, concat_axis=0, tiled=True),
        )
        sum_list.append(got_sums)
        max_list.append(got_maxima)
        total_list.append(got_totals)
    received_sums = jnp.stack(sum_list)
    received_maxima = jnp.stack(max_list)
    received_totals = jnp.stack(total_list)
    own_scores = (
        jnp.einsum("trhd,srd->trhs", queries, new_latent, preferred_element_type=jnp.float32)
        * score_scale
    )
    step_ids = jnp.arange(steps_total, dtype=jnp.int32)
    causal = step_ids[None, :] <= step_ids[:, None]
    causal_mask = causal[:, None, None, :]
    own_max = jnp.max(jnp.where(causal_mask, own_scores, neg_fill), axis=3)
    own_weights = jnp.where(causal_mask, jnp.exp(own_scores - own_max[..., None]), 0.0)
    own_total = jnp.sum(own_weights, axis=3)
    own_sum = jnp.einsum(
        "trhs,srl->trhl",
        own_weights.astype(jnp.bfloat16),
        new_latent[:, :, :latent_width],
        preferred_element_type=jnp.float32,
    )
    remote_max = received_maxima.astype(jnp.float32)
    overall = jnp.maximum(jnp.max(remote_max, axis=1), own_max)
    factor = jnp.exp(remote_max - overall[:, None])
    own_factor = jnp.exp(own_max - overall)
    numerator = (
        jnp.sum(factor[..., None] * received_sums.astype(jnp.float32), axis=1)
        + own_factor[..., None] * own_sum
    )
    denominator = (
        jnp.sum(factor * received_totals.astype(jnp.float32), axis=1) + own_factor * own_total
    )
    merged = (numerator / denominator[..., None]).astype(jnp.bfloat16)
    attention = jnp.einsum(
        "trhl,hlv->trhv", merged, w_uv, preferred_element_type=jnp.float32
    ).astype(jnp.bfloat16)
    gathered = lax.all_gather(attention, "batch", axis=1, tiled=True)
    flat_rows = gathered.reshape(
        gathered.shape[0] * gathered.shape[1], gathered.shape[2] * gathered.shape[3]
    )
    return lax.psum_scatter(
        jnp.dot(flat_rows, w_out, preferred_element_type=jnp.float32).astype(jnp.bfloat16),
        "ctx",
        scatter_dimension=0,
        tiled=True,
    )


def solution(mesh):
    return jax.shard_map(
        body,
        mesh=mesh,
        in_specs=(
            P("batch", "ctx", None),
            P(None, "batch", "ctx", None),
            P(None, "batch", None),
            P("batch"),
            P(None, "batch", None),
            P("ctx", None, None),
            P("ctx", "batch"),
        ),
        out_specs=P("ctx", "batch"),
        check_vma=False,
    )
```

profile of v0, /device:TPU:16, one launch (start us, length us, event | category | flops | bytes accessed | tf_op | source)
XLA Modules:
  0.0 756.0 jit_solution(12946825496818811959)
XLA Ops:
  12.1 87.8 %all-gather.2.cloned.1.call-done = bf16[8,2,128,576]{3,0,1,2:T(8,128)(2,1)} async-done(((bf16[8,2,4,576]{3,0,1,2:T(8,128)(2,1)}), bf16[8,2,128,576]{3,0,1,2:T(8,128)(2,1)}) %all-gather.2.cloned.1.call-update) | async-done | bytes 2359312 | tf_op jit(solution)/shard_map/all_gather | solution.py:42
  99.9 15.0 %fusion.100 = (bf16[1,2,128,576]{3,0,1,2:T(2,128)(2,1)S(1)}, bf16[1,2,128,576]{3,0,1,2:T(2,128)(2,1)}, bf16[1,2,128,576]{3,0,1,2:T(2,128)(2,1)}, bf16[1,2,128,57...) fusion(bf16[8,2,128,576]{3,0,1,2:T(8,128)(2,1)} %all-gather.2.c, ...), kind=kLoop, calls=%fused_computation.194 | loop fusion | bytes 4718592 | tf_op jit(solution)/shard_map/slice | solution.py:49
  123.7 5.8 all-to-all-start.16
  139.4 5.8 all-to-all-start
  155.2 5.2 all-to-all-start.17
  170.4 5.5 all-to-all-start.1
  185.9 5.4 all-to-all-start.18
  201.3 5.7 all-to-all-start.2
  217.0 5.6 all-to-all-start.19
  232.4 6.1 all-to-all-start.3
  248.4 5.2 all-to-all-start.20
  263.7 5.6 all-to-all-start.4
  279.3 5.3 all-to-all-start.21
  294.6 5.6 all-to-all-start.5
  304.6 5.6 all-to-all-done.5
  317.8 6.6 all-to-all-done.22
  330.5 8.0 %all-to-all-done.6 = bf16[1,2,128]{1,0,2:T(2,128)(2,1)S(1)} async-done(((bf16[1,2,128]{1,0,2:T(2,128)(2,1)}), bf16[1,2,128]{1,0,2:T(2,128)(2,1)S(1)}, u32[]{:S(2)}, u32[]{:S(2)}) %all-to-all-start.6) | async-done | bytes 544 | tf_op jit(solution)/shard_map/all_to_all | solution.py:53
  343.8 8.6 %all-to-all-done.23 = bf16[1,2,128]{1,0,2:T(2,128)(2,1)S(1)} async-done(((bf16[1,2,128]{1,0,2:T(2,128)(2,1)}), bf16[1,2,128]{1,0,2:T(2,128)(2,1)S(1)}, u32[]{:S(2)}, u32[]{:S(2)}) %all-to-all-start.23) | async-done | bytes 544 | tf_op jit(solution)/shard_map/all_to_all | solution.py:54
  359.4 7.7 %all-to-all-done.7 = bf16[1,2,128]{1,0,2:T(2,128)(2,1)S(1)} async-done(((bf16[1,2,128]{1,0,2:T(2,128)(2,1)}), bf16[1,2,128]{1,0,2:T(2,128)(2,1)S(1)}, u32[]{:S(2)}, u32[]{:S(2)}) %all-to-all-start.7) | async-done | bytes 544 | tf_op jit(solution)/shard_map/all_to_all | solution.py:53
  376.2 6.2 all-to-all-done.8
  382.4 13.9 %all-to-all-start.9 = ((bf16[1,2,128,512]{3,1,0,2:T(2,128)(2,1)}), bf16[1,2,128,512]{3,1,0,2:T(2,128)(2,1)S(1)}, u32[]{:S(2)}, u32[]{:S(2)}) async-start(bf16[1,2,128,512]{3,1,0,2:T(2,128)(2,1)} %copy.492), calls=%async_computation.9 | async-start | bytes 524288 | tf_op jit(solution)/shard_map/all_to_all | solution.py:52
  401.2 5.8 all-to-all-done.9
  416.7 5.9 all-to-all-done.10
  422.5 4.7 all-to-all-start.11
  432.2 5.8 all-to-all-done.11
  438.0 4.8 all-to-all-start.12
  463.2 9.9 %all-to-all-start.13 = ((bf16[1,2,128,512]{3,1,0,2:T(2,128)(2,1)}), bf16[1,2,128,512]{3,1,0,2:T(2,128)(2,1)}, u32[]{:S(2)}, u32[]{:S(2)}) async-start(bf16[1,2,128,512]{3,1,0,2:T(2,128)(2,1)} %copy.500), calls=%async_computation.13 | async-start | bytes 524288 | tf_op jit(solution)/shard_map/all_to_all | solution.py:52
  473.5 10.3 %all-to-all-done.13 = bf16[1,2,128,512]{3,1,0,2:T(2,128)(2,1)} async-done(((bf16[1,2,128,512]{3,1,0,2:T(2,128)(2,1)}), bf16[1,2,128,512]{3,1,0,2:T(2,128)(2,1)}, u32[]{:S(2)}, u32[]{:S(2)}) %all-to-all-start.13) | async-done | bytes 262176 | tf_op jit(solution)/shard_map/all_to_all | solution.py:52
  490.7 8.5 %all-to-all-done.14 = bf16[1,2,128,512]{3,1,0,2:T(2,128)(2,1)S(1)} async-done(((bf16[1,2,128,512]{3,1,0,2:T(2,128)(2,1)}), bf16[1,2,128,512]{3,1,0,2:T(2,128)(2,1)S(1)}, u32[]{:S(2)}, u32[]{:S(2)}) %all-to-all-start.14) | async-done | bytes 262176 | tf_op jit(solution)/shard_map/all_to_all | solution.py:52
  506.3 8.5 %all-to-all-done.15 = bf16[1,2,128,512]{3,1,0,2:T(2,128)(2,1)S(1)} async-done(((bf16[1,2,128,512]{3,1,0,2:T(2,128)(2,1)}), bf16[1,2,128,512]{3,1,0,2:T(2,128)(2,1)S(1)}, u32[]{:S(2)}, u32[]{:S(2)}) %all-to-all-start.15) | async-done | bytes 262176 | tf_op jit(solution)/shard_map/all_to_all | solution.py:52
  516.7 15.5 %all_gather.7 = bf16[8,32,4,128]{3,0,1,2:T(8,128)(2,1)S(1)} all-gather(bf16[8,2,4,128]{3,0,1,2:T(8,128)(2,1)S(1)} %fusion.15), channel_id=1, replica_groups=mesh['ctx'=32,'batch'=16] {'batch'}, dimensions={1}, use_global_device_ids=true | all-gather | bytes 278528 | tf_op jit(solution)/shard_map/all_gather | solution.py:93
  533.4 215.7 %reduce-scatter.2.cloned.1.call-done = bf16[8,448]{1,0:T(8,128)(2,1)} async-done(((bf16[256,448]{1,0:T(8,128)(2,1)}), bf16[8,448]{1,0:T(8,128)(2,1)}) %reduce-scatter.2.cloned.1.call-update) | async-done | bytes 7184 | tf_op jit(solution)/shard_map/reduce_scatter | solution.py:97
  (237 shorter events, 220.4 us)
Async XLA Ops:
  6.5 509.7 %copy-start = (bf16[4,512,128]{2,1,0:T(8,128)(2,1)S(1)}, bf16[4,512,128]{2,1,0:T(8,128)(2,1)}, u32[]{:S(2)}) copy-start(bf16[4,512,128]{2,1,0:T(8,128)(2,1)} %param.12) | copy-start | bytes 1572868
  6.5 93.4 %all-gather.2.cloned.1.call-start = ((), (), s32[]{:S(2)}) async-start(), calls=%async_computation.25 | async-start | bytes 2703360 | tf_op jit(solution)/shard_map/all_gather | solution.py:42
  123.7 15.7 %all-to-all-start.16 = ((bf16[1,2,128]{1,0,2:T(2,128)(2,1)}), bf16[1,2,128]{1,0,2:T(2,128)(2,1)}, u32[]{:S(2)}, u32[]{:S(2)}) async-start(bf16[1,2,128]{1,0,2:T(2,128)(2,1)} %copy.510), calls=%async_computation.16 | async-start | bytes 131072 | tf_op jit(solution)/shard_map/all_to_all | solution.py:54
  139.4 15.8 %all-to-all-start = ((bf16[1,2,128]{1,0,2:T(2,128)(2,1)}), bf16[1,2,128]{1,0,2:T(2,128)(2,1)}, u32[]{:S(2)}, u32[]{:S(2)}) async-start(bf16[1,2,128]{1,0,2:T(2,128)(2,1)} %copy.445), calls=%async_computation | async-start | bytes 131072 | tf_op jit(solution)/shard_map/all_to_all | solution.py:53
  155.2 15.2 %all-to-all-start.17 = ((bf16[1,2,128]{1,0,2:T(2,128)(2,1)}), bf16[1,2,128]{1,0,2:T(2,128)(2,1)}, u32[]{:S(2)}, u32[]{:S(2)}) async-start(bf16[1,2,128]{1,0,2:T(2,128)(2,1)} %copy.512), calls=%async_computation.17 | async-start | bytes 131072 | tf_op jit(solution)/shard_map/all_to_all | solution.py:54
  170.4 15.5 %all-to-all-start.1 = ((bf16[1,2,128]{1,0,2:T(2,128)(2,1)}), bf16[1,2,128]{1,0,2:T(2,128)(2,1)}, u32[]{:S(2)}, u32[]{:S(2)}) async-start(bf16[1,2,128]{1,0,2:T(2,128)(2,1)} %copy.449), calls=%async_computation.1 | async-start | bytes 131072 | tf_op jit(solution)/shard_map/all_to_all | solution.py:53
  185.9 15.4 %all-to-all-start.18 = ((bf16[1,2,128]{1,0,2:T(2,128)(2,1)}), bf16[1,2,128]{1,0,2:T(2,128)(2,1)}, u32[]{:S(2)}, u32[]{:S(2)}) async-start(bf16[1,2,128]{1,0,2:T(2,128)(2,1)} %copy.514), calls=%async_computation.18 | async-start | bytes 131072 | tf_op jit(solution)/shard_map/all_to_all | solution.py:54
  201.3 15.7 %all-to-all-start.2 = ((bf16[1,2,128]{1,0,2:T(2,128)(2,1)}), bf16[1,2,128]{1,0,2:T(2,128)(2,1)}, u32[]{:S(2)}, u32[]{:S(2)}) async-start(bf16[1,2,128]{1,0,2:T(2,128)(2,1)} %copy.453), calls=%async_computation.2 | async-start | bytes 131072 | tf_op jit(solution)/shard_map/all_to_all | solution.py:53
  217.0 15.4 %all-to-all-start.19 = ((bf16[1,2,128]{1,0,2:T(2,128)(2,1)}), bf16[1,2,128]{1,0,2:T(2,128)(2,1)}, u32[]{:S(2)}, u32[]{:S(2)}) async-start(bf16[1,2,128]{1,0,2:T(2,128)(2,1)} %copy.516), calls=%async_computation.19 | async-start | bytes 131072 | tf_op jit(solution)/shard_map/all_to_all | solution.py:54
  232.4 16.1 %all-to-all-start.3 = ((bf16[1,2,128]{1,0,2:T(2,128)(2,1)}), bf16[1,2,128]{1,0,2:T(2,128)(2,1)}, u32[]{:S(2)}, u32[]{:S(2)}) async-start(bf16[1,2,128]{1,0,2:T(2,128)(2,1)} %copy.457), calls=%async_computation.3 | async-start | bytes 131072 | tf_op jit(solution)/shard_map/all_to_all | solution.py:53
  248.4 15.2 %all-to-all-start.20 = ((bf16[1,2,128]{1,0,2:T(2,128)(2,1)}), bf16[1,2,128]{1,0,2:T(2,128)(2,1)}, u32[]{:S(2)}, u32[]{:S(2)}) async-start(bf16[1,2,128]{1,0,2:T(2,128)(2,1)} %copy.518), calls=%async_computation.20 | async-start | bytes 131072 | tf_op jit(solution)/shard_map/all_to_all | solution.py:54
  263.7 15.6 %all-to-all-start.4 = ((bf16[1,2,128]{1,0,2:T(2,128)(2,1)}), bf16[1,2,128]{1,0,2:T(2,128)(2,1)}, u32[]{:S(2)}, u32[]{:S(2)}) async-start(bf16[1,2,128]{1,0,2:T(2,128)(2,1)} %copy.461), calls=%async_computation.4 | async-start | bytes 131072 | tf_op jit(solution)/shard_map/all_to_all | solution.py:53
  279.3 15.3 %all-to-all-start.21 = ((bf16[1,2,128]{1,0,2:T(2,128)(2,1)}), bf16[1,2,128]{1,0,2:T(2,128)(2,1)}, u32[]{:S(2)}, u32[]{:S(2)}) async-start(bf16[1,2,128]{1,0,2:T(2,128)(2,1)} %copy.520), calls=%async_computation.21 | async-start | bytes 131072 | tf_op jit(solution)/shard_map/all_to_all | solution.py:54
  294.6 15.6 %all-to-all-start.5 = ((bf16[1,2,128]{1,0,2:T(2,128)(2,1)}), bf16[1,2,128]{1,0,2:T(2,128)(2,1)}, u32[]{:S(2)}, u32[]{:S(2)}) async-start(bf16[1,2,128]{1,0,2:T(2,128)(2,1)} %copy.465), calls=%async_computation.5 | async-start | bytes 131072 | tf_op jit(solution)/shard_map/all_to_all | solution.py:53
  310.2 14.1 %all-to-all-start.22 = ((bf16[1,2,128]{1,0,2:T(2,128)(2,1)}), bf16[1,2,128]{1,0,2:T(2,128)(2,1)S(1)}, u32[]{:S(2)}, u32[]{:S(2)}) async-start(bf16[1,2,128]{1,0,2:T(2,128)(2,1)} %copy.522), calls=%async_computation.22 | async-start | bytes 131072 | tf_op jit(solution)/shard_map/all_to_all | solution.py:54
  314.3 28.1 %copy-start.16 = (bf16[8,2,576]{2,1,0:T(2,128)(2,1)S(1)}, bf16[8,2,576]{2,1,0:T(2,128)(2,1)}, u32[]{:S(2)}) copy-start(bf16[8,2,576]{2,1,0:T(2,128)(2,1)} %param.9) | copy-start | bytes 55300
  314.3 41.9 %copy-start.11 = (pred[2,1024]{1,0:T(4,128)(4,1)S(1)}, pred[2,1024]{1,0:T(4,128)(4,1)}, u32[]{:S(2)}) copy-start(pred[2,1024]{1,0:T(4,128)(4,1)} %get-tuple-element.42) | copy-start | bytes 6148
  314.3 41.9 %copy-start.21 = (f32[2,128]{1,0:T(2,128)S(1)}, f32[2,128]{1,0:T(2,128)}, u32[]{:S(2)}) copy-start(f32[2,128]{1,0:T(2,128)} %copy-done.20) | copy-start | bytes 3076
  324.3 14.2 %all-to-all-start.6 = ((bf16[1,2,128]{1,0,2:T(2,128)(2,1)}), bf16[1,2,128]{1,0,2:T(2,128)(2,1)S(1)}, u32[]{:S(2)}, u32[]{:S(2)}) async-start(bf16[1,2,128]{1,0,2:T(2,128)(2,1)} %copy.469), calls=%async_computation.6 | async-start | bytes 131072 | tf_op jit(solution)/shard_map/all_to_all | solution.py:53
  338.5 13.8 %all-to-all-start.23 = ((bf16[1,2,128]{1,0,2:T(2,128)(2,1)}), bf16[1,2,128]{1,0,2:T(2,128)(2,1)S(1)}, u32[]{:S(2)}, u32[]{:S(2)}) async-start(bf16[1,2,128]{1,0,2:T(2,128)(2,1)} %copy.524), calls=%async_computation.23 | async-start | bytes 131072 | tf_op jit(solution)/shard_map/all_to_all | solution.py:54
  342.4 29.2 %copy-start.26 = (pred[8,8]{0,1:T(8,128)(4,1)}, pred[8,8]{0,1:T(8,128)(4,1)S(1)}, u32[]{:S(2)}) copy-start(pred[8,8]{0,1:T(8,128)(4,1)S(1)} %iota_compare_fusion) | copy-start | bytes 196
  352.4 14.7 %all-to-all-start.7 = ((bf16[1,2,128]{1,0,2:T(2,128)(2,1)}), bf16[1,2,128]{1,0,2:T(2,128)(2,1)S(1)}, u32[]{:S(2)}, u32[]{:S(2)}) async-start(bf16[1,2,128]{1,0,2:T(2,128)(2,1)} %copy.473), calls=%async_computation.7 | async-start | bytes 131072 | tf_op jit(solution)/shard_map/all_to_all | solution.py:53
  367.7 14.7 %all-to-all-start.8 = ((bf16[1,2,128,512]{3,1,0,2:T(2,128)(2,1)}), bf16[1,2,128,512]{3,1,0,2:T(2,128)(2,1)S(1)}, u32[]{:S(2)}, u32[]{:S(2)}) async-start(bf16[1,2,128,512]{3,1,0,2:T(2,128)(2,1)} %copy.490), calls=%async_computation.8 | async-start | bytes 524288 | tf_op jit(solution)/shard_map/all_to_all | solution.py:52
  382.4 24.7 %all-to-all-start.9 = ((bf16[1,2,128,512]{3,1,0,2:T(2,128)(2,1)}), bf16[1,2,128,512]{3,1,0,2:T(2,128)(2,1)S(1)}, u32[]{:S(2)}, u32[]{:S(2)}) async-start(bf16[1,2,128,512]{3,1,0,2:T(2,128)(2,1)} %copy.492), calls=%async_computation.9 | async-start | bytes 524288 | tf_op jit(solution)/shard_map/all_to_all | solution.py:52
  407.1 15.4 %all-to-all-start.10 = ((bf16[1,2,128,512]{3,1,0,2:T(2,128)(2,1)}), bf16[1,2,128,512]{3,1,0,2:T(2,128)(2,1)}, u32[]{:S(2)}, u32[]{:S(2)}) async-start(bf16[1,2,128,512]{3,1,0,2:T(2,128)(2,1)} %copy.494), calls=%async_computation.10 | async-start | bytes 524288 | tf_op jit(solution)/shard_map/all_to_all | solution.py:52
  422.5 15.5 %all-to-all-start.11 = ((bf16[1,2,128,512]{3,1,0,2:T(2,128)(2,1)}), bf16[1,2,128,512]{3,1,0,2:T(2,128)(2,1)}, u32[]{:S(2)}, u32[]{:S(2)}) async-start(bf16[1,2,128,512]{3,1,0,2:T(2,128)(2,1)} %copy.496), calls=%async_computation.11 | async-start | bytes 524288 | tf_op jit(solution)/shard_map/all_to_all | solution.py:52
  438.0 25.1 %all-to-all-start.12 = ((bf16[1,2,128,512]{3,1,0,2:T(2,128)(2,1)}), bf16[1,2,128,512]{3,1,0,2:T(2,128)(2,1)}, u32[]{:S(2)}, u32[]{:S(2)}) async-start(bf16[1,2,128,512]{3,1,0,2:T(2,128)(2,1)} %copy.498), calls=%async_computation.12 | async-start | bytes 524288 | tf_op jit(solution)/shard_map/all_to_all | solution.py:52
  444.9 28.3 %copy-start.13 = (f32[8,2,4]{0,2,1:T(4,128)S(1)}, f32[8,2,4]{0,2,1:T(4,128)}, u32[]{:S(2)}) copy-start(f32[8,2,4]{0,2,1:T(4,128)} %get-tuple-element.24) | copy-start | bytes 772
  463.2 20.6 %all-to-all-start.13 = ((bf16[1,2,128,512]{3,1,0,2:T(2,128)(2,1)}), bf16[1,2,128,512]{3,1,0,2:T(2,128)(2,1)}, u32[]{:S(2)}, u32[]{:S(2)}) async-start(bf16[1,2,128,512]{3,1,0,2:T(2,128)(2,1)} %copy.500), calls=%async_computation.13 | async-start | bytes 524288 | tf_op jit(solution)/shard_map/all_to_all | solution.py:52
  483.8 15.5 %all-to-all-start.14 = ((bf16[1,2,128,512]{3,1,0,2:T(2,128)(2,1)}), bf16[1,2,128,512]{3,1,0,2:T(2,128)(2,1)S(1)}, u32[]{:S(2)}, u32[]{:S(2)}) async-start(bf16[1,2,128,512]{3,1,0,2:T(2,128)(2,1)} %copy.502), calls=%async_computation.14 | async-start | bytes 524288 | tf_op jit(solution)/shard_map/all_to_all | solution.py:52
  499.3 15.5 %all-to-all-start.15 = ((bf16[1,2,128,512]{3,1,0,2:T(2,128)(2,1)}), bf16[1,2,128,512]{3,1,0,2:T(2,128)(2,1)S(1)}, u32[]{:S(2)}, u32[]{:S(2)}) async-start(bf16[1,2,128,512]{3,1,0,2:T(2,128)(2,1)} %copy.504), calls=%async_computation.15 | async-start | bytes 524288 | tf_op jit(solution)/shard_map/all_to_all | solution.py:52
  503.9 245.2 %reduce-scatter.2.cloned.1.call-start = ((), (), s32[]{:S(2)}) async-start(), calls=%async_computation.26 | async-start | bytes 270336 | tf_op jit(solution)/shard_map/reduce_scatter | solution.py:97
  (21 other events, 204.8 us)
Sparse Core Ops, SparseCore 0:
  10.5 89.3 all-gather.1
  533.5 215.5 reduce-scatter.1
where the time goes:
time: 768 us; the launch traced here: 756 us
  waiting for transfers between devices  439 us (57%)
  starting transfers between devices  133 us (17%)
  local copies, waits for them, and re-layouts  85.7 us (11%)
  matrix products  40.8 us (5%)
  other arithmetic  27.6 us (4%)
  blocking collectives  15.5 us (2%)
  between operations  14.1 us (2%)
    reduce_scatter x1, waiting for transfers between devices, body(): lax.psum_scatter(jnp.dot(flat_rows, w_out, preferred_element_type=jnp.flo...  216 us
    all_gather x1, waiting for transfers between devices, body(): all_queries = lax.all_gather(queries, 'ctx', axis=2, tiled=True)  87.8 us
    all_to_all x8, starting transfers between devices, body(): lax.all_to_all(summed[None], 'ctx', split_axis=2, concat_axis=0, tiled=True)  51 us
    all_to_all x8, waiting for transfers between devices, body(): lax.all_to_all(summed[None], 'ctx', split_axis=2, concat_axis=0, tiled=True)  51 us
    all_to_all x8, waiting for transfers between devices, body(): lax.all_to_all(maxima[None], 'ctx', split_axis=2, concat_axis=0, tiled=True)  44.2 us
    all_to_all x8, starting transfers between devices, body(): lax.all_to_all(maxima[None], 'ctx', split_axis=2, concat_axis=0, tiled=True)  41.9 us
    all_to_all x8, starting transfers between devices, body(): lax.all_to_all(totals[None], 'ctx', split_axis=2, concat_axis=0, tiled=True)  40.5 us
    all_to_all x8, waiting for transfers between devices, body(): lax.all_to_all(totals[None], 'ctx', split_axis=2, concat_axis=0, tiled=True)  40.1 us
  transfers between devices with their start and end apart: 26, of which 25 were waited for; matrix products, arithmetic and copies ran while one was open for 16% of the time, Pallas kernels for 0%

commit v1 on v0

v1 whole, which is shorter than its diff:
```python
import functools

import jax
import jax.numpy as jnp
from jax import lax
from jax.experimental import pallas as pl
from jax.experimental.pallas import tpu as pltpu
from jax.sharding import Mesh, PartitionSpec as P

BLOCK = 64
X_SIZE = 4
Z_SIZE = 8
STEPS = 8
LOG2E = 1.4426950408889634
DEAD = -1e30
FLOOR = -1e20
score_scale = 192.0 ** (-0.5)

MIB = 2**20


def params(mib):
    return pltpu.CompilerParams(vmem_limit_bytes=mib * MIB)


def matmul(a, b):
    return jnp.dot(a, b, preferred_element_type=jnp.float32)


def matmul_t(a, b):
    return lax.dot_general(a, b, (((1,), (1,)), ((), ())), preferred_element_type=jnp.float32)


def iota(shape, axis):
    return lax.broadcasted_iota(jnp.int32, shape, axis)


def pack_kernel(q_ref, out_ref):
    count = q_ref.shape[0]
    half = count // 2
    blocks = [q_ref[:, k * 128 : (k + 1) * 128] for k in range(4)]
    rope = q_ref[:, 512:576].astype(jnp.float32)
    wide = jnp.concatenate([rope, rope], axis=1)
    rope = jnp.where(iota((half, 128), 1) < 64, wide[:half], wide[half:]).astype(jnp.bfloat16)
    for z in range(out_ref.shape[0]):
        for k in range(4):
            out_ref[z, k * count : (k + 1) * count, :] = blocks[k]
        out_ref[z, 4 * count :, :] = rope


def pack(q_rows, copies):
    count = q_rows.shape[0]
    return pl.pallas_call(
        pack_kernel,
        out_shape=jax.ShapeDtypeStruct((copies, 4 * count + count // 2, 128), jnp.bfloat16),
        compiler_params=params(8),
        name="pack_queries",
    )(q_rows)


def unpack(refs, r):
    length = refs[0].shape[1]
    count = length * 2 // 9
    half = count // 2
    blocks = []
    for k in range(4):
        at = slice(k * count + r * half, k * count + (r + 1) * half)
        blocks.append(jnp.concatenate([ref[z, at, :] for ref in refs for z in range(ref.shape[0])]))
    latent = jnp.concatenate(blocks, axis=1)
    at = slice(4 * count, 4 * count + half)
    rope = jnp.concatenate([ref[z, at, :] for ref in refs for z in range(ref.shape[0])])
    return latent, rope


def beside(rope, r):
    blank = jnp.zeros_like(rope)
    return jnp.concatenate([rope, blank] if r == 0 else [blank, rope], axis=0)


def partial_kernel(*refs):
    q_refs, (keys_ref, bias_ref, out_ref, cols) = refs[:-4], refs[-4:]
    zs = sum(ref.shape[0] for ref in q_refs)
    chunk = q_refs[0].shape[1] * 2 // 9
    half = chunk // 2
    count = zs * half
    for r in range(2):
        latent, rope = unpack(q_refs, r)
        values = keys_ref[r, :512, :]
        scores = matmul(latent, values) + matmul(rope, beside(keys_ref[r, 512:, :], r))
        bias = bias_ref[r]
        scores = (scores.reshape(count // STEPS, STEPS, -1) + bias[None]).reshape(count, -1)
        top = jnp.maximum(jnp.max(scores, axis=1, keepdims=True) * score_scale, FLOOR)
        top = top.astype(jnp.bfloat16).astype(jnp.float32)
        weights = jnp.exp2(scores * (score_scale * LOG2E) - top * LOG2E)
        total = jnp.sum(weights, axis=1, keepdims=True)
        summed = matmul_t(weights.astype(jnp.bfloat16), values).astype(jnp.bfloat16)
        lanes = iota((count, 128), 1)
        meta = jnp.where(lanes == 0, top, jnp.where(lanes == 1, total, 0.0))
        for z in range(zs):
            at = z * chunk + r * half
            part = slice(z * half, (z + 1) * half)
            out_ref[at : at + half, :] = summed[part]
            cols[at : at + half, :] = meta[part]
    end = zs * chunk
    out_ref[end : end + 16, :] = cols[...].T[:16].astype(jnp.bfloat16)


def local_partial(q_chunks, keys, bias):
    chunk = q_chunks[0].shape[1] * 2 // 9
    queries = sum(q.shape[0] for q in q_chunks) * chunk
    return pl.pallas_call(
        partial_kernel,
        out_shape=jax.ShapeDtypeStruct((queries + 16, 512), jnp.bfloat16),
        scratch_shapes=[pltpu.VMEM((queries, 128), jnp.float32)],
        compiler_params=params(32),
        cost_estimate=pl.CostEstimate(
            flops=2 * queries * keys.shape[2] * 1152,
            bytes_accessed=4 * MIB,
            transcendentals=queries * keys.shape[2],
        ),
        name="local_partial",
    )(*q_chunks, keys, bias)


def combine_kernel(a_ref, b_ref, c_ref, d_ref, out_ref):
    refs = (a_ref, b_ref, c_ref, d_ref)
    zs = out_ref.shape[0]
    chunk = (a_ref.shape[0] - 16) // zs
    count = zs * chunk
    metas = [ref[count : count + 16, :].astype(jnp.float32) for ref in refs]
    tops = [meta[0:1] for meta in metas]
    top = functools.reduce(jnp.maximum, tops)
    factors = [jnp.exp(one - top) for one in tops]
    total = sum(f * meta[1:2] for f, meta in zip(factors, metas))
    place = iota((128, count), 0)
    stacked = jnp.zeros((128, count), jnp.float32)
    for i, f in enumerate(factors):
        stacked = jnp.where(place == i, f, stacked)
    cols = stacked.T
    place = iota((16, count), 0)
    meta = jnp.where(place == 0, top, jnp.where(place == 1, total, 0.0))
    for z in range(zs):
        rows = slice(z * chunk, (z + 1) * chunk)
        merged = sum(
            cols[rows, i : i + 1] * ref[rows, :].astype(jnp.float32) for i, ref in enumerate(refs)
        ).astype(jnp.bfloat16)
        for k in range(4):
            out_ref[z, k * chunk : (k + 1) * chunk, :] = merged[:, k * 128 : (k + 1) * 128]
        tile = meta[:, (z // 2) * 128 : (z // 2 + 1) * 128]
        if z % 2:
            tile = pltpu.roll(tile, 64, 1)
        out_ref[z, 4 * chunk : 4 * chunk + 16, :] = tile.astype(jnp.bfloat16)


def combine(parts, zs, chunk):
    return pl.pallas_call(
        combine_kernel,
        out_shape=jax.ShapeDtypeStruct((zs, 4 * chunk + 16, 128), jnp.bfloat16),
        compiler_params=params(16),
        name="combine_x",
    )(*parts)


def own_kernel(q_ref, fresh_ref, bias_ref, sum_ref, meta_ref):
    half = sum_ref.shape[0] // 2
    for r in range(2):
        latent, rope = unpack([q_ref], r)
        fresh = fresh_ref[r]
        scores = matmul_t(latent, fresh[:, :512])
        wide = jnp.concatenate([fresh[:, 512:].astype(jnp.float32)] * 2, axis=1)
        mine = (iota(wide.shape, 1) < 64) == (r == 0)
        scores = scores + matmul_t(rope, jnp.where(mine, wide, 0.0).astype(jnp.bfloat16))
        scores = (scores.reshape(half // STEPS, STEPS, -1) + bias_ref[...][None]).reshape(half, -1)
        top = jnp.max(scores, axis=1, keepdims=True) * score_scale
        weights = jnp.exp2(scores * (score_scale * LOG2E) - top * LOG2E)
        total = jnp.sum(weights, axis=1, keepdims=True)
        at = slice(r * half, (r + 1) * half)
        sum_ref[at, :] = matmul(weights.astype(jnp.bfloat16), fresh[:, :512])
        lanes = iota((half, 128), 1)
        meta_ref[at, :] = jnp.where(lanes == 0, top, jnp.where(lanes == 1, total, 0.0))


def own_part(packed, fresh, causal):
    length = packed.shape[1]
    count = length * 2 // 9
    return pl.pallas_call(
        own_kernel,
        grid=(1,),
        in_specs=[
            pl.BlockSpec((1, length, 128), lambda i: (0, 0, 0)),
            pl.BlockSpec(fresh.shape, lambda i: (0, 0, 0)),
            pl.BlockSpec(causal.shape, lambda i: (0, 0)),
        ],
        out_specs=[
            pl.BlockSpec((count, 512), lambda i: (0, 0)),
            pl.BlockSpec((count, 128), lambda i: (0, 0)),
        ],
        out_shape=(
            jax.ShapeDtypeStruct((count, 512), jnp.float32),
            jax.ShapeDtypeStruct((count, 128), jnp.float32),
        ),
        compiler_params=params(8),
        name="own_part",
    )(packed, fresh, causal)


def merge_kernel(got_ref, sum_ref, meta_ref, up_ref, out_ref):
    zs = got_ref.shape[0]
    count = sum_ref.shape[0]
    heads = up_ref.shape[0]
    rows = count // (heads * STEPS)
    place = iota((128, 128), 0)
    stacked = jnp.zeros((128, 128), jnp.float32)
    for z in range(zs):
        meta = got_ref[z, 4 * count : 4 * count + 16, :].astype(jnp.float32)
        stacked = jnp.where(place == z, meta[0:1], stacked)
        stacked = jnp.where(place == zs + z, meta[1:2], stacked)
    cols = stacked.T[:count]
    tops, totals = cols[:, :zs], cols[:, zs : 2 * zs]
    own_top, own_total = meta_ref[:, 0:1], meta_ref[:, 1:2]
    top = jnp.maximum(jnp.max(tops, axis=1, keepdims=True), own_top)
    factors = jnp.exp(tops - top)
    own_factor = jnp.exp(own_top - top)
    bottom = jnp.sum(factors * totals, axis=1, keepdims=True) + own_factor * own_total
    pieces = []
    for k in range(4):
        piece = own_factor * sum_ref[:, k * 128 : (k + 1) * 128]
        for z in range(zs):
            block = got_ref[z, k * count : (k + 1) * count, :].astype(jnp.float32)
            piece = piece + factors[:, z : z + 1] * block
        pieces.append(piece / bottom)
    merged = jnp.concatenate(pieces, axis=1)
    for h in range(heads):
        mine = jnp.concatenate(
            [merged[(r * heads + h) * STEPS : (r * heads + h + 1) * STEPS] for r in range(rows)]
        ).astype(jnp.bfloat16)
        lifted = matmul(mine, up_ref[h]).astype(jnp.bfloat16)
        for copy in range(out_ref.shape[0]):
            out_ref[copy, :, h * 128 : (h + 1) * 128] = lifted


def merge(got, own_sum, own_meta, w_uv, copies):
    shape = (copies, own_sum.shape[0] // w_uv.shape[0], w_uv.shape[0] * w_uv.shape[2])
    return pl.pallas_call(
        merge_kernel,
        out_shape=jax.ShapeDtypeStruct(shape, jnp.bfloat16),
        compiler_params=params(16),
        name="merge_up",
    )(got, own_sum, own_meta, w_uv)


def project_kernel(rows_ref, w_ref, out_ref):
    n = rows_ref.shape[0]
    to, come = iota((n, n), 0), iota((n, n), 1)
    rows = n // STEPS
    here = (to % rows) * STEPS + to // rows == come
    here = here.astype(jnp.float32).astype(jnp.bfloat16)
    ordered = matmul(here, rows_ref[...]).astype(jnp.bfloat16)
    out_ref[...] = matmul_t(ordered, w_ref[...]).astype(jnp.bfloat16)


def project(rows, w_out_t):
    return pl.pallas_call(
        project_kernel,
        out_shape=jax.ShapeDtypeStruct((rows.shape[0], w_out_t.shape[0]), jnp.bfloat16),
        compiler_params=params(16),
        name="project_out",
    )(rows, w_out_t)


def shift(value, axis, by, size):
    return lax.ppermute(value, axis, [(i, (i + by) % size) for i in range(size)])


def after(value, earlier):
    return lax.optimization_barrier((value, earlier))[0]


def swap_all(value, axis):
    return lax.all_to_all(value, axis, split_axis=0, concat_axis=0, tiled=True)


def body(latent_cache, queries, new_latent, lengths, selection, w_uv, w_out):
    steps, rows, heads, width = queries.shape
    keys = latent_cache.shape[1]
    shard = lax.axis_index("x") * Z_SIZE + lax.axis_index("z")

    q_rows = jnp.transpose(queries, (1, 2, 0, 3)).reshape(rows * heads * steps, width)
    packed = pack(q_rows, Z_SIZE)
    line = swap_all(packed, "z")
    far = shift(line, "x", 2, X_SIZE)
    left = shift(line, "x", 1, X_SIZE)
    right = shift(line, "x", -1, X_SIZE)

    blocks = shard * (keys // BLOCK) + jnp.arange(keys // BLOCK, dtype=jnp.int32)
    chosen = jnp.any(selection[:, :, :, None] == blocks, axis=2)
    positions = shard * keys + jnp.arange(keys, dtype=jnp.int32)
    live = jnp.repeat(chosen, BLOCK, axis=2) & (positions < lengths[:, None])[None]
    bias = jnp.where(jnp.transpose(live, (1, 0, 2)), 0.0, DEAD)
    cache_t = jnp.transpose(latent_cache, (0, 2, 1))

    ids = jnp.arange(128, dtype=jnp.int32)
    causal = jnp.where(ids[None, :] <= jnp.arange(steps)[:, None], 0.0, DEAD)
    fresh = jnp.pad(jnp.transpose(new_latent, (1, 0, 2)), ((0, 0), (0, 128 - steps), (0, 0)))
    own_sum, own_meta = own_part(packed, fresh, causal)

    here = local_partial([line], cache_t, bias)
    for_left = local_partial([after(left, here)], cache_t, bias)
    for_right = local_partial([right], cache_t, bias)
    for_far = local_partial([far], cache_t, bias)
    parts = [
        here,
        shift(for_left, "x", -1, X_SIZE),
        shift(for_right, "x", 1, X_SIZE),
        shift(for_far, "x", 2, X_SIZE),
    ]
    got = swap_all(combine(parts, Z_SIZE, rows * heads * steps), "z")
    groups = lax.axis_size(("y", "core"))
    attention = swap_all(merge(got, own_sum, own_meta, w_uv, groups), ("y", "core"))
    shares = project(attention.reshape(groups * rows * steps, -1), w_out.T)
    shares = shares.reshape(X_SIZE * Z_SIZE, -1, shares.shape[1])
    got_shares = swap_all(shares, ("x", "z"))
    return jnp.sum(got_shares.astype(jnp.float32), axis=0).astype(jnp.bfloat16)


def solution(mesh):
    batch = mesh.shape["batch"]
    fine = Mesh(mesh.devices.reshape(X_SIZE, Z_SIZE, batch // 2, 2), ("x", "z", "y", "core"))
    ctx, rows = ("x", "z"), ("y", "core")
    return jax.shard_map(
        body,
        mesh=fine,
        in_specs=(
            P(rows, ctx, None),
            P(None, rows, ctx, None),
            P(None, rows, None),
            P(rows),
            P(None, rows, None),
            P(ctx, None, None),
            P(ctx, rows),
        ),
        out_specs=P(ctx, rows),
        check_vma=False,
    )
```

time: 768 us -> 147 us (0.19)
  the two profiles are of different devices: /device:TPU:16 before, /device:TPU:64 now
where the time goes in v1:
time: 147 us; the launch traced here: 146 us
  waiting for transfers between devices  52.9 us (36%)
  starting transfers between devices  37.8 us (26%)
  blocking collectives  37.2 us (25%)
  Pallas kernels  13 us (9%)
  local copies, waits for them, and re-layouts  2.83 us (2%)
  other arithmetic  2.53 us (2%)
    all_to_all x2, blocking collectives, swap_all(): return lax.all_to_all(value, axis, split_axis=0, concat_axis=0, tiled=True)  37.2 us
    all_to_all x2, waiting for transfers between devices, swap_all(): return lax.all_to_all(value, axis, split_axis=0, concat_axis=0, tiled=True)  32.1 us
    ppermute x6, starting transfers between devices, shift(): lax.ppermute(value, axis, [(i, (i + by) % size) for i in range(size)])  22.9 us
    ppermute x6, waiting for transfers between devices, shift(): lax.ppermute(value, axis, [(i, (i + by) % size) for i in range(size)])  20.8 us
    all_to_all x2, starting transfers between devices, swap_all(): return lax.all_to_all(value, axis, split_axis=0, concat_axis=0, tiled=True)  14.9 us
    pallas_call x4, Pallas kernels, local_partial(): pl.pallas_call(partial_kernel, out_shape=jax.ShapeDtypeStruct((queries +...  7.85 us
  transfers between devices with their start and end apart: 8, of which 6 were waited for; matrix products, arithmetic and copies ran while one was open for 1% of the time, Pallas kernels for 6%

profile of v1, /device:TPU:64, one launch (start us, length us, event | category | flops | bytes accessed | tf_op | source)
XLA Modules:
  0.0 146.5 jit_solution(4668293430689898746)
XLA Ops:
  0.0 0.9 copy.10
  0.9 0.9 pack_queries.1.q_ref
  1.8 10.0 %all-to-all-start = ((bf16[8,288,128]{2,1,0:T(8,128)(2,1)}), bf16[8,288,128]{2,1,0:T(8,128)(2,1)S(1)}, u32[]{:S(2)}, u32[]{:S(2)}) async-start(bf16[8,288,128]{2,1,0:T(8,128)(2,1)} %pack_queries.1.q_ref), calls=%async_computation | async-start | bytes 1179648 | tf_op jit(solution)/shard_map/all_to_all | solution.py:280
  11.8 17.4 %all-to-all-done.refs_0_ = bf16[8,288,128]{2,1,0:T(8,128)(2,1)S(1)} async-done(((bf16[8,288,128]{2,1,0:T(8,128)(2,1)}), bf16[8,288,128]{2,1,0:T(8,128)(2,1)S(1)}, u32[]{:S(2)}, u32[]{:S(2)}) %all-to-all-start) | async-done | bytes 589856 | tf_op jit(solution)/shard_map/all_to_all | solution.py:280
  29.2 4.9 %collective-permute-start.4 = (bf16[8,288,128]{2,1,0:T(8,128)(2,1)S(1)}, bf16[8,288,128]{2,1,0:T(8,128)(2,1)S(1)}, u32[]{:S(2)}, u32[]{:S(2)}) collective-permute-start(bf16[8,288,128]{2,1,0:T(8,128)(2,1)S(1)} %all-to-all-done.refs_0_), channel_id=1, source_target_pairs={{0,256},{128,384},{256,0},{384,128},{1,257},{129,385},{257,1},{385... | collective-permute-start | bytes 1769480 | tf_op jit(solution)/shard_map/ppermute | solution.py:272
  34.1 0.7 broadcast_compare_fusion
  34.9 3.0 %collective-permute-start.2 = (bf16[8,288,128]{2,1,0:T(8,128)(2,1)S(1)}, bf16[8,288,128]{2,1,0:T(8,128)(2,1)S(1)}, u32[]{:S(2)}, u32[]{:S(2)}) collective-permute-start(bf16[8,288,128]{2,1,0:T(8,128)(2,1)S(1)} %all-to-all-done.refs_0_), channel_id=1, source_target_pairs={{0,384},{128,0},{256,128},{384,256},{1,385},{129,1},{257,129},{385... | collective-permute-start | bytes 1769480 | tf_op jit(solution)/shard_map/ppermute | solution.py:272
  37.9 2.8 %collective-permute-start = (bf16[8,288,128]{2,1,0:T(8,128)(2,1)S(1)}, bf16[8,288,128]{2,1,0:T(8,128)(2,1)S(1)}, u32[]{:S(2)}, u32[]{:S(2)}) collective-permute-start(bf16[8,288,128]{2,1,0:T(8,128)(2,1)S(1)} %all-to-all-done.refs_0_), channel_id=1, source_target_pairs={{0,128},{128,256},{256,384},{384,0},{1,129},{129,257},{257,385},{3... | collective-permute-start | bytes 1769480 | tf_op jit(solution)/shard_map/ppermute | solution.py:272
  40.7 1.1 compare_reduce_fusion
  41.9 0.1 broadcast_in_dim.26
  42.0 0.1 reshape.48
  42.1 1.7 %copy-done.2 = bf16[2,1024,576]{1,2,0:T(8,128)(2,1)S(1)} copy-done((bf16[2,1024,576]{1,2,0:T(8,128)(2,1)S(1)}, bf16[2,1024,576]{1,2,0:T(8,128)(2,1)}, u32[]{:S(2)}) %copy-start.2) | copy-done | bytes 2359320
  43.8 2.0 %local_partial.4.a_ref = bf16[528,512]{1,0:T(8,128)(2,1)S(1)} custom-call(bf16[8,288,128]{2,1,0:T(8,128)(2,1)S(1)} %all-to-all-done.refs_0_, bf16[2,576,1024]{2,1,0:T(8,128)(2,1)S(1)} %bitcast.19, f32[2,8,1024]{2,1,0:T(8,128)S(1)} %select_bitcast_fusion.refs_2_), custom_call_target="tpu_custom_call" | custom-call | flops 1207959552 | bytes 4194304 | tf_op jit(solution)/shard_map/local_partial/pallas_call | solution.py:111
  45.8 3.1 %collective-permute-done.4.refs_0_ = bf16[8,288,128]{2,1,0:T(8,128)(2,1)S(1)} collective-permute-done((bf16[8,288,128]{2,1,0:T(8,128)(2,1)S(1)}, bf16[8,288,128]{2,1,0:T(8,128)(2,1)S(1)}, u32[]{:S(2)}, u32[]{:S(2)}) %collective-permute-start.4) | collective-permute-done | bytes 589856 | tf_op jit(solution)/shard_map/ppermute | solution.py:272
  48.9 2.0 %local_partial.7 = bf16[528,512]{1,0:T(8,128)(2,1)S(1)} custom-call(bf16[8,288,128]{2,1,0:T(8,128)(2,1)S(1)} %collective-permute-done.4.refs_0_, bf16[2,576,1024]{2,1,0:T(8,128)(2,1)S(1)} %bitcast.20, f32[2,8,1024]{2,1,0:T(8,128)S(1)} %select_bitcast_fusion.refs_2_), custom_call_target="tpu_custom_call" | custom-call | flops 1207959552 | bytes 4194304 | tf_op jit(solution)/shard_map/local_partial/pallas_call | solution.py:111
  50.8 5.0 %collective-permute-start.5 = (bf16[528,512]{1,0:T(8,128)(2,1)S(1)}, bf16[528,512]{1,0:T(8,128)(2,1)S(1)}, u32[]{:S(2)}, u32[]{:S(2)}) collective-permute-start(bf16[528,512]{1,0:T(8,128)(2,1)S(1)} %local_partial.7), channel_id=1, source_target_pairs={{0,256},{128,384},{256,0},{384,128},{1,257},{129,385},{257,1},{385... | collective-permute-start | bytes 1622024 | tf_op jit(solution)/shard_map/ppermute | solution.py:272
  55.8 5.8 %collective-permute-done.2.refs_0_ = bf16[8,288,128]{2,1,0:T(8,128)(2,1)S(1)} collective-permute-done((bf16[8,288,128]{2,1,0:T(8,128)(2,1)S(1)}, bf16[8,288,128]{2,1,0:T(8,128)(2,1)S(1)}, u32[]{:S(2)}, u32[]{:S(2)}) %collective-permute-start.2) | collective-permute-done | bytes 589856 | tf_op jit(solution)/shard_map/ppermute | solution.py:272
  61.6 2.0 %local_partial.6 = bf16[528,512]{1,0:T(8,128)(2,1)S(1)} custom-call(bf16[8,288,128]{2,1,0:T(8,128)(2,1)S(1)} %collective-permute-done.2.refs_0_, bf16[2,576,1024]{2,1,0:T(8,128)(2,1)S(1)} %bitcast.21, f32[2,8,1024]{2,1,0:T(8,128)S(1)} %select_bitcast_fusion.refs_2_), custom_call_target="tpu_custom_call" | custom-call | flops 1207959552 | bytes 4194304 | tf_op jit(solution)/shard_map/local_partial/pallas_call | solution.py:111
  63.6 3.2 %collective-permute-start.3 = (bf16[528,512]{1,0:T(8,128)(2,1)S(1)}, bf16[528,512]{1,0:T(8,128)(2,1)S(1)}, u32[]{:S(2)}, u32[]{:S(2)}) collective-permute-start(bf16[528,512]{1,0:T(8,128)(2,1)S(1)} %local_partial.6), channel_id=1, source_target_pairs={{0,128},{128,256},{256,384},{384,0},{1,129},{129,257},{257,385},{3... | collective-permute-start | bytes 1622024 | tf_op jit(solution)/shard_map/ppermute | solution.py:272
  66.8 2.0 %local_partial.5 = bf16[528,512]{1,0:T(8,128)(2,1)S(1)} custom-call(bf16[8,288,128]{2,1,0:T(8,128)(2,1)S(1)} %collective-permute-done.refs_0_, bf16[2,576,1024]{2,1,0:T(8,128)(2,1)S(1)} %bitcast.22, f32[2,8,1024]{2,1,0:T(8,128)S(1)} %select_bitcast_fusion.refs_2_), custom_call_target="tpu_custom_call" | custom-call | flops 1207959552 | bytes 4194304 | tf_op jit(solution)/shard_map/local_partial/pallas_call | solution.py:111
  68.8 4.0 %collective-permute-start.1 = (bf16[528,512]{1,0:T(8,128)(2,1)S(1)}, bf16[528,512]{1,0:T(8,128)(2,1)S(1)}, u32[]{:S(2)}, u32[]{:S(2)}) collective-permute-start(bf16[528,512]{1,0:T(8,128)(2,1)S(1)} %local_partial.5), channel_id=1, source_target_pairs={{0,384},{128,0},{256,128},{384,256},{1,385},{129,1},{257,129},{385... | collective-permute-start | bytes 1622024 | tf_op jit(solution)/shard_map/ppermute | solution.py:272
  72.8 7.9 %collective-permute-done.3.c_ref = bf16[528,512]{1,0:T(8,128)(2,1)S(1)} collective-permute-done((bf16[528,512]{1,0:T(8,128)(2,1)S(1)}, bf16[528,512]{1,0:T(8,128)(2,1)S(1)}, u32[]{:S(2)}, u32[]{:S(2)}) %collective-permute-start.3) | collective-permute-done | bytes 540704 | tf_op jit(solution)/shard_map/ppermute | solution.py:272
  80.7 4.0 %collective-permute-done.1.b_ref = bf16[528,512]{1,0:T(8,128)(2,1)S(1)} collective-permute-done((bf16[528,512]{1,0:T(8,128)(2,1)S(1)}, bf16[528,512]{1,0:T(8,128)(2,1)S(1)}, u32[]{:S(2)}, u32[]{:S(2)}) %collective-permute-start.1) | collective-permute-done | bytes 540704 | tf_op jit(solution)/shard_map/ppermute | solution.py:272
  84.7 1.5 %combine_x.1 = bf16[8,272,128]{2,1,0:T(8,128)(2,1)} custom-call(bf16[528,512]{1,0:T(8,128)(2,1)S(1)} %local_partial.4.a_ref, bf16[528,512]{1,0:T(8,128)(2,1)S(1)} %collective-permute-done.1.b_ref, bf16[528,512]{1,0:T(8,128)(2,1)S(1)} %collective-permute-done.3.c_ref, bf16[528,512]{1,0:T(8,128)(2,1)S(1)} %collective-permute-done.5.d_ref), custom_call_target="tpu_custom_call" | custom-call | tf_op jit(solution)/shard_map/combine_x/pallas_call | solution.py:156
  86.2 5.0 %all-to-all-start.1 = ((bf16[8,272,128]{2,1,0:T(8,128)(2,1)}), bf16[8,272,128]{2,1,0:T(8,128)(2,1)S(1)}, u32[]{:S(2)}, u32[]{:S(2)}) async-start(bf16[8,272,128]{2,1,0:T(8,128)(2,1)} %combine_x.1), calls=%async_computation.1 | async-start | bytes 1114112 | tf_op jit(solution)/shard_map/all_to_all | solution.py:280
  91.2 1.6 %own_part.1 = (f32[64,512]{1,0:T(8,128)S(1)}, f32[64,128]{1,0:T(8,128)S(1)}) custom-call(bf16[8,288,128]{2,1,0:T(8,128)(2,1)} %pack_queries.1.q_ref, bf16[2,128,576]{2,1,0:T(8,128)(2,1)S(1)} %pad.4.fresh_ref, f32[8,128]{1,0:T(8,128)S(1)} %fusion.bias_ref), custom_call_target="tpu_custom_call" | custom-call | tf_op jit(solution)/shard_map/own_part/pallas_call | solution.py:186
  92.8 14.6 %all-to-all-done.1.got_ref = bf16[8,272,128]{2,1,0:T(8,128)(2,1)S(1)} async-done(((bf16[8,272,128]{2,1,0:T(8,128)(2,1)}), bf16[8,272,128]{2,1,0:T(8,128)(2,1)S(1)}, u32[]{:S(2)}, u32[]{:S(2)}) %all-to-all-start.1) | async-done | bytes 557088 | tf_op jit(solution)/shard_map/all_to_all | solution.py:280
  107.4 0.7 merge_up.1
  108.2 18.2 %all_to_all.20 = bf16[16,16,512]{2,1,0:T(8,128)(2,1)S(1)} all-to-all(bf16[16,16,512]{2,1,0:T(8,128)(2,1)S(1)} %merge_up.1), channel_id=1, replica_groups=mesh['x'=4,'z'=8,'y'=8,'core'=2] {'y','core'}, dimensions={0} | all-to-all | bytes 524288 | tf_op jit(solution)/shard_map/all_to_all | solution.py:280
  126.4 0.4 project_out.1
  126.8 19.0 %all_to_all.21 = bf16[32,8,448]{2,1,0:T(8,128)(2,1)S(1)} all-to-all(bf16[32,8,448]{2,1,0:T(8,128)(2,1)S(1)} %bitcast.16), channel_id=1, replica_groups=mesh['x'=4,'z'=8,'y'=8,'core'=2] {'x','z'}, dimensions={0} | all-to-all | bytes 458752 | tf_op jit(solution)/shard_map/all_to_all | solution.py:280
  145.8 0.7 reduce_sum.12
  (16 shorter events, 0.1 us)
Async XLA Ops:
  1.8 27.4 %all-to-all-start = ((bf16[8,288,128]{2,1,0:T(8,128)(2,1)}), bf16[8,288,128]{2,1,0:T(8,128)(2,1)S(1)}, u32[]{:S(2)}, u32[]{:S(2)}) async-start(bf16[8,288,128]{2,1,0:T(8,128)(2,1)} %pack_queries.1.q_ref), calls=%async_computation | async-start | bytes 1179648 | tf_op jit(solution)/shard_map/all_to_all | solution.py:280
  29.2 19.7 %collective-permute-start.4 = (bf16[8,288,128]{2,1,0:T(8,128)(2,1)S(1)}, bf16[8,288,128]{2,1,0:T(8,128)(2,1)S(1)}, u32[]{:S(2)}, u32[]{:S(2)}) collective-permute-start(bf16[8,288,128]{2,1,0:T(8,128)(2,1)S(1)} %all-to-all-done.refs_0_), channel_id=1, source_target_pairs={{0,256},{128,384},{256,0},{384,128},{1,257},{129,385},{257,1},{385... | collective-permute-start | bytes 1769480 | tf_op jit(solution)/shard_map/ppermute | solution.py:272
  34.9 26.8 %collective-permute-start.2 = (bf16[8,288,128]{2,1,0:T(8,128)(2,1)S(1)}, bf16[8,288,128]{2,1,0:T(8,128)(2,1)S(1)}, u32[]{:S(2)}, u32[]{:S(2)}) collective-permute-start(bf16[8,288,128]{2,1,0:T(8,128)(2,1)S(1)} %all-to-all-done.refs_0_), channel_id=1, source_target_pairs={{0,384},{128,0},{256,128},{384,256},{1,385},{129,1},{257,129},{385... | collective-permute-start | bytes 1769480 | tf_op jit(solution)/shard_map/ppermute | solution.py:272
  37.9 28.9 %collective-permute-start = (bf16[8,288,128]{2,1,0:T(8,128)(2,1)S(1)}, bf16[8,288,128]{2,1,0:T(8,128)(2,1)S(1)}, u32[]{:S(2)}, u32[]{:S(2)}) collective-permute-start(bf16[8,288,128]{2,1,0:T(8,128)(2,1)S(1)} %all-to-all-done.refs_0_), channel_id=1, source_target_pairs={{0,128},{128,256},{256,384},{384,0},{1,129},{129,257},{257,385},{3... | collective-permute-start | bytes 1769480 | tf_op jit(solution)/shard_map/ppermute | solution.py:272
  42.1 1.7 %copy-start.2 = (bf16[2,1024,576]{1,2,0:T(8,128)(2,1)S(1)}, bf16[2,1024,576]{1,2,0:T(8,128)(2,1)}, u32[]{:S(2)}) copy-start(bf16[2,1024,576]{1,2,0:T(8,128)(2,1)} %param.7) | copy-start | bytes 7077892
  50.8 22.0 %collective-permute-start.5 = (bf16[528,512]{1,0:T(8,128)(2,1)S(1)}, bf16[528,512]{1,0:T(8,128)(2,1)S(1)}, u32[]{:S(2)}, u32[]{:S(2)}) collective-permute-start(bf16[528,512]{1,0:T(8,128)(2,1)S(1)} %local_partial.7), channel_id=1, source_target_pairs={{0,256},{128,384},{256,0},{384,128},{1,257},{129,385},{257,1},{385... | collective-permute-start | bytes 1622024 | tf_op jit(solution)/shard_map/ppermute | solution.py:272
  63.6 17.1 %collective-permute-start.3 = (bf16[528,512]{1,0:T(8,128)(2,1)S(1)}, bf16[528,512]{1,0:T(8,128)(2,1)S(1)}, u32[]{:S(2)}, u32[]{:S(2)}) collective-permute-start(bf16[528,512]{1,0:T(8,128)(2,1)S(1)} %local_partial.6), channel_id=1, source_target_pairs={{0,128},{128,256},{256,384},{384,0},{1,129},{129,257},{257,385},{3... | collective-permute-start | bytes 1622024 | tf_op jit(solution)/shard_map/ppermute | solution.py:272
  68.8 22.3 %copy-start.3 = (bf16[8,2,576]{2,1,0:T(2,128)(2,1)S(1)}, bf16[8,2,576]{2,1,0:T(2,128)(2,1)}, u32[]{:S(2)}) copy-start(bf16[8,2,576]{2,1,0:T(2,128)(2,1)} %param.9) | copy-start | bytes 55300
  68.8 38.6 %copy-start = (bf16[4,512,128]{2,1,0:T(8,128)(2,1)S(1)}, bf16[4,512,128]{2,1,0:T(8,128)(2,1)}, u32[]{:S(2)}) copy-start(bf16[4,512,128]{2,1,0:T(8,128)(2,1)} %up_ref.1) | copy-start | bytes 1572868
  68.8 15.9 %collective-permute-start.1 = (bf16[528,512]{1,0:T(8,128)(2,1)S(1)}, bf16[528,512]{1,0:T(8,128)(2,1)S(1)}, u32[]{:S(2)}, u32[]{:S(2)}) collective-permute-start(bf16[528,512]{1,0:T(8,128)(2,1)S(1)} %local_partial.5), channel_id=1, source_target_pairs={{0,384},{128,0},{256,128},{384,256},{1,385},{129,1},{257,129},{385... | collective-permute-start | bytes 1622024 | tf_op jit(solution)/shard_map/ppermute | solution.py:272
  86.2 40.2 %copy-start.1 = (bf16[512,448]{0,1:T(8,128)(2,1)S(1)}, bf16[512,448]{0,1:T(8,128)(2,1)}, u32[]{:S(2)}) copy-start(bf16[512,448]{0,1:T(8,128)(2,1)} %param.13) | copy-start | bytes 1376260
  86.2 21.3 %all-to-all-start.1 = ((bf16[8,272,128]{2,1,0:T(8,128)(2,1)}), bf16[8,272,128]{2,1,0:T(8,128)(2,1)S(1)}, u32[]{:S(2)}, u32[]{:S(2)}) async-start(bf16[8,272,128]{2,1,0:T(8,128)(2,1)} %combine_x.1), calls=%async_computation.1 | async-start | bytes 1114112 | tf_op jit(solution)/shard_map/all_to_all | solution.py:280

commit v2 on v1

--- a/solution.py
+++ b/solution.py
@@ -35,41 +35,65 @@
     return lax.broadcasted_iota(jnp.int32, shape, axis)
 
 
-def pack_kernel(q_ref, out_ref):
-    count = q_ref.shape[0]
-    half = count // 2
-    blocks = [q_ref[:, k * 128 : (k + 1) * 128] for k in range(4)]
+PART = 16
+FEW, MANY = 5 * PART, 14 * PART
+
+
+def pack_kernel(q_ref, few_ref, many_ref):
     rope = q_ref[:, 512:576].astype(jnp.float32)
     wide = jnp.concatenate([rope, rope], axis=1)
-    rope = jnp.where(iota((half, 128), 1) < 64, wide[:half], wide[half:]).astype(jnp.bfloat16)
-    for z in range(out_ref.shape[0]):
-        for k in range(4):
-            out_ref[z, k * count : (k + 1) * count, :] = blocks[k]
-        out_ref[z, 4 * count :, :] = rope
+    low = iota((PART, 128), 1) < 64
+    quarter = [wide[i * PART : (i + 1) * PART] for i in range(4)]
+    first = jnp.where(low, quarter[0], 0.0).astype(jnp.bfloat16)
+    second = jnp.where(low, quarter[1], quarter[2]).astype(jnp.bfloat16)
+    third = jnp.where(low, 0.0, quarter[3]).astype(jnp.bfloat16)
+    for k in range(4):
+        lanes = slice(k * 128, (k + 1) * 128)
+        few_ref[k * PART : (k + 1) * PART, :] = q_ref[:PART, lanes]
+        for z in range(many_ref.shape[0]):
+            many_ref[z, 3 * k * PART : 3 * (k + 1) * PART, :] = q_ref[PART:, lanes]
+    few_ref[4 * PART :, :] = first
+    for z in range(many_ref.shape[0]):
+        many_ref[z, 12 * PART : 13 * PART, :] = second
+        many_ref[z, 13 * PART :, :] = third
 
 
 def pack(q_rows, copies):
-    count = q_rows.shape[0]
     return pl.pallas_call(
         pack_kernel,
-        out_shape=jax.ShapeDtypeStruct((copies, 4 * count + count // 2, 128), jnp.bfloat16),
+        out_shape=(
+            jax.ShapeDtypeStruct((FEW, 128), jnp.bfloat16),
+            jax.ShapeDtypeStruct((copies, MANY, 128), jnp.bfloat16),
+        ),
         compiler_params=params(8),
         name="pack_queries",
     )(q_rows)
 
 
-def unpack(refs, r):
-    length = refs[0].shape[1]
-    count = length * 2 // 9
-    half = count // 2
-    blocks = []
-    for k in range(4):
-        at = slice(k * count + r * half, k * count + (r + 1) * half)
-        blocks.append(jnp.concatenate([ref[z, at, :] for ref in refs for z in range(ref.shape[0])]))
-    latent = jnp.concatenate(blocks, axis=1)
-    at = slice(4 * count, 4 * count + half)
-    rope = jnp.concatenate([ref[z, at, :] for ref in refs for z in range(ref.shape[0])])
-    return latent, rope
+def unpack(few, many, r, zs):
+    def gather(get, at, size):
+        return [get(z, at, size) for z in range(zs)]
+
+    if r == 0:
+        blocks = [
+            gather(few, k * PART, PART) + gather(many, 3 * k * PART, PART) for k in range(4)
+        ]
+        rope = gather(few, 4 * PART, PART) + gather(many, 12 * PART, PART)
+    else:
+        blocks = [gather(many, (3 * k + 1) * PART, 2 * PART) for k in range(4)]
+        rope = gather(many, 12 * PART, 2 * PART)
+    latent = jnp.concatenate([jnp.concatenate(block) for block in blocks], axis=1)
+    return latent, jnp.concatenate(rope)
+
+
+def spread(r, zs):
+    if r == 0:
+        for half in range(2):
+            for z in range(zs):
+                yield (half * zs + z) * PART, z * 4 * PART + half * PART, PART
+    else:
+        for z in range(zs):
+            yield z * 2 * PART, (z * 4 + 2) * PART, 2 * PART
 
 
 def beside(rope, r):
@@ -77,14 +101,16 @@
     return jnp.concatenate([rope, blank] if r == 0 else [blank, rope], axis=0)
 
 
-def partial_kernel(*refs):
-    q_refs, (keys_ref, bias_ref, out_ref, cols) = refs[:-4], refs[-4:]
-    zs = sum(ref.shape[0] for ref in q_refs)
-    chunk = q_refs[0].shape[1] * 2 // 9
-    half = chunk // 2
-    count = zs * half
+def partial_kernel(place, few_ref, many_ref, keys_ref, bias_ref, out_ref, cols):
+    zs = many_ref.shape[0]
+    count = zs * 2 * PART
     for r in range(2):
-        latent, rope = unpack(q_refs, r)
+        latent, rope = unpack(
+            lambda z, at, size: few_ref[z, place, at : at + size, :],
+            lambda z, at, size: many_ref[z, at : at + size, :],
+            r,
+            zs,
+        )
         values = keys_ref[r, :512, :]
         scores = matmul(latent, values) + matmul(rope, beside(keys_ref[r, 512:, :], r))
         bias = bias_ref[r]
@@ -96,20 +122,17 @@
         summed = matmul_t(weights.astype(jnp.bfloat16), values).astype(jnp.bfloat16)
         lanes = iota((count, 128), 1)
         meta = jnp.where(lanes == 0, top, jnp.where(lanes == 1, total, 0.0))
-        for z in range(zs):
-            at = z * chunk + r * half
-            part = slice(z * half, (z + 1) * half)
-            out_ref[at : at + half, :] = summed[part]
-            cols[at : at + half, :] = meta[part]
-    end = zs * chunk
+        for come, to, size in spread(r, zs):
+            out_ref[to : to + size, :] = summed[come : come + size]
+            cols[to : to + size, :] = meta[come : come + size]
+    end = zs * 4 * PART
     out_ref[end : end + 16, :] = cols[...].T[:16].astype(jnp.bfloat16)
 
 
-def local_partial(q_chunks, keys, bias):
-    chunk = q_chunks[0].shape[1] * 2 // 9
-    queries = sum(q.shape[0] for q in q_chunks) * chunk
-    return pl.pallas_call(
-        partial_kernel,
+def local_partial(place, few, many, keys, bias):
+    queries = many.shape[0] * 4 * PART
+    return pl.pallas_call(
+        functools.partial(partial_kernel, place),
         out_shape=jax.ShapeDtypeStruct((queries + 16, 512), jnp.bfloat16),
         scratch_shapes=[pltpu.VMEM((queries, 128), jnp.float32)],
         compiler_params=params(32),
@@ -119,7 +142,7 @@
             transcendentals=queries * keys.shape[2],
         ),
         name="local_partial",
-    )(*q_chunks, keys, bias)
+    )(few, many, keys, bias)
 
 
 def combine_kernel(a_ref, b_ref, c_ref, d_ref, out_ref):
@@ -161,10 +184,15 @@
     )(*parts)
 
 
-def own_kernel(q_ref, fresh_ref, bias_ref, sum_ref, meta_ref):
+def own_kernel(few_ref, many_ref, fresh_ref, bias_ref, sum_ref, meta_ref):
     half = sum_ref.shape[0] // 2
     for r in range(2):
-        latent, rope = unpack([q_ref], r)
+        latent, rope = unpack(
+            lambda z, at, size: few_ref[at : at + size, :],
+            lambda z, at, size: many_ref[z, at : at + size, :],
+            r,
+            1,
+        )
         fresh = fresh_ref[r]
         scores = matmul_t(latent, fresh[:, :512])
         wide = jnp.concatenate([fresh[:, 512:].astype(jnp.float32)] * 2, axis=1)
@@ -180,14 +208,14 @@
         meta_ref[at, :] = jnp.where(lanes == 0, top, jnp.where(lanes == 1, total, 0.0))
 
 
-def own_part(packed, fresh, causal):
-    length = packed.shape[1]
-    count = length * 2 // 9
+def own_part(few, many, fresh, causal):
+    count = 4 * PART
     return pl.pallas_call(
         own_kernel,
         grid=(1,),
         in_specs=[
-            pl.BlockSpec((1, length, 128), lambda i: (0, 0, 0)),
+            pl.BlockSpec(few.shape, lambda i: (0, 0)),
+            pl.BlockSpec((1, MANY, 128), lambda i: (0, 0, 0)),
             pl.BlockSpec(fresh.shape, lambda i: (0, 0, 0)),
             pl.BlockSpec(causal.shape, lambda i: (0, 0)),
         ],
@@ -201,7 +229,7 @@
         ),
         compiler_params=params(8),
         name="own_part",
-    )(packed, fresh, causal)
+    )(few, many, fresh, causal)
 
 
 def merge_kernel(got_ref, sum_ref, meta_ref, up_ref, out_ref):
@@ -286,8 +314,12 @@
     shard = lax.axis_index("x") * Z_SIZE + lax.axis_index("z")
 
     q_rows = jnp.transpose(queries, (1, 2, 0, 3)).reshape(rows * heads * steps, width)
-    packed = pack(q_rows, Z_SIZE)
-    line = swap_all(packed, "z")
+    few, many = pack(q_rows, Z_SIZE)
+    line = swap_all(many, "z")
+    cross = jnp.stack([few] + [shift(few, "x", d, X_SIZE) for d in range(1, X_SIZE)])
+    cross = jnp.broadcast_to(cross[None], (Z_SIZE,) + cross.shape)
+    line, cross = lax.optimization_barrier((line, cross))
+    cross = swap_all(cross, "z")
     far = shift(line, "x", 2, X_SIZE)
     left = shift(line, "x", 1, X_SIZE)
     right = shift(line, "x", -1, X_SIZE)
@@ -302,12 +334,12 @@
     ids = jnp.arange(128, dtype=jnp.int32)
     causal = jnp.where(ids[None, :] <= jnp.arange(steps)[:, None], 0.0, DEAD)
     fresh = jnp.pad(jnp.transpose(new_latent, (1, 0, 2)), ((0, 0), (0, 128 - steps), (0, 0)))
-    own_sum, own_meta = own_part(packed, fresh, causal)
-
-    here = local_partial([line], cache_t, bias)
-    for_left = local_partial([after(left, here)], cache_t, bias)
-    for_right = local_partial([right], cache_t, bias)
-    for_far = local_partial([far], cache_t, bias)
+    own_sum, own_meta = own_part(few, many, fresh, causal)
+
+    here = local_partial(0, cross, line, cache_t, bias)
+    for_left = local_partial(1, cross, left, cache_t, bias)
+    for_right = local_partial(3, cross, right, cache_t, bias)
+    for_far = local_partial(2, cross, after(far, here), cache_t, bias)
     parts = [
         here,
         shift(for_left, "x", -1, X_SIZE),

time: 147 us -> 150 us (1.020)
  starting transfers between devices: 37.8 us -> 54.8 us
  waiting for transfers between devices: 52.9 us -> 38.4 us
    all_to_all x2 -> x3, waiting for transfers between devices: 32.1 us -> 21.1 us  [swap_all(): return lax.all_to_all(value, axis, split_axis=0, concat_axis=0, tiled=True)]
    ppermute x6 -> x9, starting transfers between devices: 22.9 us -> 31.5 us  [shift(): lax.ppermute(value, axis, [(i, (i + by) % size) for i in range(size)])]
    all_to_all x2 -> x3, starting transfers between devices: 14.9 us -> 23.2 us  [swap_all(): return lax.all_to_all(value, axis, split_axis=0, concat_axis=0, tiled=True)]
    ppermute x6 -> x9, waiting for transfers between devices: 20.8 us -> 17.3 us  [shift(): lax.ppermute(value, axis, [(i, (i + by) % size) for i in range(size)])]
  transfers between devices with their start and end apart: 8 -> 12, of which waited for: 6 -> 6; matrix products, arithmetic and copies ran while one was open for 1% -> 1% of each run, Pallas kernels for 6% -> 6%
where the time goes in v2:
time: 150 us; the launch traced here: 149 us
  starting transfers between devices  54.8 us (37%)
  waiting for transfers between devices  38.4 us (26%)
  blocking collectives  37.7 us (25%)
  Pallas kernels  12.9 us (9%)
  local copies, waits for them, and re-layouts  3.81 us (3%)
    all_to_all x2, blocking collectives, swap_all(): return lax.all_to_all(value, axis, split_axis=0, concat_axis=0, tiled=True)  37.7 us
    ppermute x9, starting transfers between devices, shift(): lax.ppermute(value, axis, [(i, (i + by) % size) for i in range(size)])  31.5 us
    all_to_all x3, starting transfers between devices, swap_all(): return lax.all_to_all(value, axis, split_axis=0, concat_axis=0, tiled=True)  23.2 us
    all_to_all x3, waiting for transfers between devices, swap_all(): return lax.all_to_all(value, axis, split_axis=0, concat_axis=0, tiled=True)  21.1 us
    ppermute x9, waiting for transfers between devices, shift(): lax.ppermute(value, axis, [(i, (i + by) % size) for i in range(size)])  17.3 us
    pallas_call x4, Pallas kernels, local_partial(): pl.pallas_call(functools.partial(partial_kernel, place), out_shape=jax.Sh...  7.85 us
  transfers between devices with their start and end apart: 12, of which 6 were waited for; matrix products, arithmetic and copies ran while one was open for 1% of the time, Pallas kernels for 6%

profile of v2, /device:TPU:64, one launch (start us, length us, event | category | flops | bytes accessed | tf_op | source)
XLA Modules:
  0.0 149.0 jit_solution(8986570054264901362)
XLA Ops:
  0.0 0.9 copy.10
  0.9 0.8 pack_queries.1
  1.8 10.0 %all-to-all-start = ((bf16[8,224,128]{2,1,0:T(8,128)(2,1)}), bf16[8,224,128]{2,1,0:T(8,128)(2,1)S(1)}, u32[]{:S(2)}, u32[]{:S(2)}) async-start(bf16[8,224,128]{2,1,0:T(8,128)(2,1)} %get-tuple-element.12.many_ref), calls=%async_computation | async-start | bytes 917504 | tf_op jit(solution)/shard_map/all_to_all | solution.py:308
  11.7 4.7 %collective-permute-start.2 = (bf16[80,128]{1,0:T(8,128)(2,1)S(1)}, bf16[80,128]{1,0:T(8,128)(2,1)S(1)}, u32[]{:S(2)}, u32[]{:S(2)}) collective-permute-start(bf16[80,128]{1,0:T(8,128)(2,1)S(1)} %get-tuple-element.13.few_ref), channel_id=1, source_target_pairs={{0,384},{128,0},{256,128},{384,256},{1,385},{129,1},{257,129},{385... | collective-permute-start | bytes 61448 | tf_op jit(solution)/shard_map/ppermute | solution.py:300
  16.4 2.7 %collective-permute-start.1 = (bf16[80,128]{1,0:T(8,128)(2,1)S(1)}, bf16[80,128]{1,0:T(8,128)(2,1)S(1)}, u32[]{:S(2)}, u32[]{:S(2)}) collective-permute-start(bf16[80,128]{1,0:T(8,128)(2,1)S(1)} %get-tuple-element.13.few_ref), channel_id=1, source_target_pairs={{0,256},{128,384},{256,0},{384,128},{1,257},{129,385},{257,1},{385... | collective-permute-start | bytes 61448 | tf_op jit(solution)/shard_map/ppermute | solution.py:300
  19.1 2.8 %collective-permute-start = (bf16[80,128]{1,0:T(8,128)(2,1)S(1)}, bf16[80,128]{1,0:T(8,128)(2,1)S(1)}, u32[]{:S(2)}, u32[]{:S(2)}) collective-permute-start(bf16[80,128]{1,0:T(8,128)(2,1)S(1)} %get-tuple-element.13.few_ref), channel_id=1, source_target_pairs={{0,128},{128,256},{256,384},{384,0},{1,129},{129,257},{257,385},{3... | collective-permute-start | bytes 61448 | tf_op jit(solution)/shard_map/ppermute | solution.py:300
  21.9 1.9 %collective-permute-done.1 = bf16[80,128]{1,0:T(8,128)(2,1)S(1)} collective-permute-done((bf16[80,128]{1,0:T(8,128)(2,1)S(1)}, bf16[80,128]{1,0:T(8,128)(2,1)S(1)}, u32[]{:S(2)}, u32[]{:S(2)}) %collective-permute-start.1) | collective-permute-done | bytes 20512 | tf_op jit(solution)/shard_map/ppermute | solution.py:300
  23.9 2.2 %collective-permute-done = bf16[80,128]{1,0:T(8,128)(2,1)S(1)} collective-permute-done((bf16[80,128]{1,0:T(8,128)(2,1)S(1)}, bf16[80,128]{1,0:T(8,128)(2,1)S(1)}, u32[]{:S(2)}, u32[]{:S(2)}) %collective-permute-start) | collective-permute-done | bytes 20512 | tf_op jit(solution)/shard_map/ppermute | solution.py:300
  26.4 0.9 broadcast_in_dim.32
  27.3 6.9 %all-to-all-start.1 = ((bf16[8,4,80,128]{3,2,1,0:T(8,128)(2,1)}), bf16[8,4,80,128]{3,2,1,0:T(8,128)(2,1)S(1)}, u32[]{:S(2)}, u32[]{:S(2)}) async-start(bf16[8,4,80,128]{3,2,1,0:T(8,128)(2,1)} %broadcast_in_dim.32), calls=%async_computation.1 | async-start | bytes 1310720 | tf_op jit(solution)/shard_map/all_to_all | solution.py:308
  34.3 3.4 %collective-permute-start.7 = (bf16[8,224,128]{2,1,0:T(8,128)(2,1)S(1)}, bf16[8,224,128]{2,1,0:T(8,128)(2,1)S(1)}, u32[]{:S(2)}, u32[]{:S(2)}) collective-permute-start(bf16[8,224,128]{2,1,0:T(8,128)(2,1)S(1)} %all-to-all-done.many_ref), channel_id=1, source_target_pairs={{0,256},{128,384},{256,0},{384,128},{1,257},{129,385},{257,1},{385... | collective-permute-start | bytes 1376264 | tf_op jit(solution)/shard_map/ppermute | solution.py:300
  37.7 2.0 %collective-permute-start.3 = (bf16[8,224,128]{2,1,0:T(8,128)(2,1)S(1)}, bf16[8,224,128]{2,1,0:T(8,128)(2,1)S(1)}, u32[]{:S(2)}, u32[]{:S(2)}) collective-permute-start(bf16[8,224,128]{2,1,0:T(8,128)(2,1)S(1)} %all-to-all-done.many_ref), channel_id=1, source_target_pairs={{0,128},{128,256},{256,384},{384,0},{1,129},{129,257},{257,385},{3... | collective-permute-start | bytes 1376264 | tf_op jit(solution)/shard_map/ppermute | solution.py:300
  39.8 0.4 compare_reduce_fusion
  40.4 5.0 %collective-permute-start.5 = (bf16[8,224,128]{2,1,0:T(8,128)(2,1)S(1)}, bf16[8,224,128]{2,1,0:T(8,128)(2,1)S(1)}, u32[]{:S(2)}, u32[]{:S(2)}) collective-permute-start(bf16[8,224,128]{2,1,0:T(8,128)(2,1)S(1)} %all-to-all-done.many_ref), channel_id=1, source_target_pairs={{0,384},{128,0},{256,128},{384,256},{1,385},{129,1},{257,129},{385... | collective-permute-start | bytes 1376264 | tf_op jit(solution)/shard_map/ppermute | solution.py:300
  45.5 6.0 %all-to-all-done.1.few_ref = bf16[8,4,80,128]{3,2,1,0:T(8,128)(2,1)S(1)} async-done(((bf16[8,4,80,128]{3,2,1,0:T(8,128)(2,1)}), bf16[8,4,80,128]{3,2,1,0:T(8,128)(2,1)S(1)}, u32[]{:S(2)}, u32[]{:S(2)}) %all-to-all-start.1) | async-done | bytes 655392 | tf_op jit(solution)/shard_map/all_to_all | solution.py:308
  51.5 1.7 %copy-done.2 = bf16[2,1024,576]{1,2,0:T(8,128)(2,1)S(1)} copy-done((bf16[2,1024,576]{1,2,0:T(8,128)(2,1)S(1)}, bf16[2,1024,576]{1,2,0:T(8,128)(2,1)}, u32[]{:S(2)}) %copy-start.2) | copy-done | bytes 2359320
  53.1 2.0 %local_partial.4.a_ref = bf16[528,512]{1,0:T(8,128)(2,1)S(1)} custom-call(bf16[8,4,80,128]{3,2,1,0:T(8,128)(2,1)S(1)} %all-to-all-done.1.few_ref, bf16[8,224,128]{2,1,0:T(8,128)(2,1)S(1)} %all-to-all-done.many_ref, bf16[2,576,1024]{2,1,0:T(8,128)(2,1)S(1)} %bitcast.24, f32[2,8,1024]{2,1,0:T(8,128)S(1)} %select_bitcast_fusion.bias_ref), custom_call_target="tpu_custom_call" | custom-call | flops 1207959552 | bytes 4194304 | tf_op jit(solution)/shard_map/local_partial/pallas_call | solution.py:134
  55.1 2.0 %local_partial.7 = bf16[528,512]{1,0:T(8,128)(2,1)S(1)} custom-call(bf16[8,4,80,128]{3,2,1,0:T(8,128)(2,1)S(1)} %all-to-all-done.1.few_ref, bf16[8,224,128]{2,1,0:T(8,128)(2,1)S(1)} %collective-permute-done.7.many_ref, bf16[2,576,1024]{2,1,0:T(8,128)(2,1)S(1)} %bitcast.25, f32[2,8,1024]{2,1,0:T(8,128)S(1)} %select_bitcast_fusion.bias_ref), custom_call_target="tpu_custom_call" | custom-call | flops 1207959552 | bytes 4194304 | tf_op jit(solution)/shard_map/local_partial/pallas_call | solution.py:134
  57.1 4.9 %collective-permute-start.8 = (bf16[528,512]{1,0:T(8,128)(2,1)S(1)}, bf16[528,512]{1,0:T(8,128)(2,1)S(1)}, u32[]{:S(2)}, u32[]{:S(2)}) collective-permute-start(bf16[528,512]{1,0:T(8,128)(2,1)S(1)} %local_partial.7), channel_id=1, source_target_pairs={{0,256},{128,384},{256,0},{384,128},{1,257},{129,385},{257,1},{385... | collective-permute-start | bytes 1622024 | tf_op jit(solution)/shard_map/ppermute | solution.py:300
  62.0 2.0 %local_partial.5 = bf16[528,512]{1,0:T(8,128)(2,1)S(1)} custom-call(bf16[8,4,80,128]{3,2,1,0:T(8,128)(2,1)S(1)} %all-to-all-done.1.few_ref, bf16[8,224,128]{2,1,0:T(8,128)(2,1)S(1)} %collective-permute-done.3.many_ref, bf16[2,576,1024]{2,1,0:T(8,128)(2,1)S(1)} %bitcast.26, f32[2,8,1024]{2,1,0:T(8,128)S(1)} %select_bitcast_fusion.bias_ref), custom_call_target="tpu_custom_call" | custom-call | flops 1207959552 | bytes 4194304 | tf_op jit(solution)/shard_map/local_partial/pallas_call | solution.py:134
  64.0 3.1 %collective-permute-start.4 = (bf16[528,512]{1,0:T(8,128)(2,1)S(1)}, bf16[528,512]{1,0:T(8,128)(2,1)S(1)}, u32[]{:S(2)}, u32[]{:S(2)}) collective-permute-start(bf16[528,512]{1,0:T(8,128)(2,1)S(1)} %local_partial.5), channel_id=1, source_target_pairs={{0,384},{128,0},{256,128},{384,256},{1,385},{129,1},{257,129},{385... | collective-permute-start | bytes 1622024 | tf_op jit(solution)/shard_map/ppermute | solution.py:300
  67.1 2.0 %local_partial.6 = bf16[528,512]{1,0:T(8,128)(2,1)S(1)} custom-call(bf16[8,4,80,128]{3,2,1,0:T(8,128)(2,1)S(1)} %all-to-all-done.1.few_ref, bf16[8,224,128]{2,1,0:T(8,128)(2,1)S(1)} %collective-permute-done.5.many_ref, bf16[2,576,1024]{2,1,0:T(8,128)(2,1)S(1)} %bitcast.27, f32[2,8,1024]{2,1,0:T(8,128)S(1)} %select_bitcast_fusion.bias_ref), custom_call_target="tpu_custom_call" | custom-call | flops 1207959552 | bytes 4194304 | tf_op jit(solution)/shard_map/local_partial/pallas_call | solution.py:134
  69.1 2.9 %collective-permute-start.6 = (bf16[528,512]{1,0:T(8,128)(2,1)S(1)}, bf16[528,512]{1,0:T(8,128)(2,1)S(1)}, u32[]{:S(2)}, u32[]{:S(2)}) collective-permute-start(bf16[528,512]{1,0:T(8,128)(2,1)S(1)} %local_partial.6), channel_id=1, source_target_pairs={{0,128},{128,256},{256,384},{384,0},{1,129},{129,257},{257,385},{3... | collective-permute-start | bytes 1622024 | tf_op jit(solution)/shard_map/ppermute | solution.py:300
  72.0 13.2 %collective-permute-done.4.b_ref = bf16[528,512]{1,0:T(8,128)(2,1)S(1)} collective-permute-done((bf16[528,512]{1,0:T(8,128)(2,1)S(1)}, bf16[528,512]{1,0:T(8,128)(2,1)S(1)}, u32[]{:S(2)}, u32[]{:S(2)}) %collective-permute-start.4) | collective-permute-done | bytes 540704 | tf_op jit(solution)/shard_map/ppermute | solution.py:300
  85.2 1.5 combine_x.1
  86.7 6.4 %all-to-all-start.2 = ((bf16[8,272,128]{2,1,0:T(8,128)(2,1)}), bf16[8,272,128]{2,1,0:T(8,128)(2,1)S(1)}, u32[]{:S(2)}, u32[]{:S(2)}) async-start(bf16[8,272,128]{2,1,0:T(8,128)(2,1)} %combine_x.1), calls=%async_computation.2 | async-start | bytes 1114112 | tf_op jit(solution)/shard_map/all_to_all | solution.py:308
  93.2 1.6 %own_part.1 = (f32[64,512]{1,0:T(8,128)S(1)}, f32[64,128]{1,0:T(8,128)S(1)}) custom-call(bf16[80,128]{1,0:T(8,128)(2,1)S(1)} %get-tuple-element.13.few_ref, bf16[8,224,128]{2,1,0:T(8,128)(2,1)} %get-tuple-element.12.many_ref, bf16[2,128,576]{2,1,0:T(8,128)(2,1)S(1)} %pad.4.fresh_ref, f32[8,128]{1,0:T(8,128)S(1)} %fusion.bias_ref), custom_call_target="tpu_custom_call" | custom-call | tf_op jit(solution)/shard_map/own_part/pallas_call | solution.py:213
  94.7 14.8 %all-to-all-done.2.got_ref = bf16[8,272,128]{2,1,0:T(8,128)(2,1)S(1)} async-done(((bf16[8,272,128]{2,1,0:T(8,128)(2,1)}), bf16[8,272,128]{2,1,0:T(8,128)(2,1)S(1)}, u32[]{:S(2)}, u32[]{:S(2)}) %all-to-all-start.2) | async-done | bytes 557088 | tf_op jit(solution)/shard_map/all_to_all | solution.py:308
  109.5 0.7 merge_up.1
  110.3 18.2 %all_to_all.25 = bf16[16,16,512]{2,1,0:T(8,128)(2,1)S(1)} all-to-all(bf16[16,16,512]{2,1,0:T(8,128)(2,1)S(1)} %merge_up.1), channel_id=1, replica_groups=mesh['x'=4,'z'=8,'y'=8,'core'=2] {'y','core'}, dimensions={0} | all-to-all | bytes 524288 | tf_op jit(solution)/shard_map/all_to_all | solution.py:308
  128.9 19.5 %all_to_all.26 = bf16[32,8,448]{2,1,0:T(8,128)(2,1)S(1)} all-to-all(bf16[32,8,448]{2,1,0:T(8,128)(2,1)S(1)} %bitcast.20), channel_id=1, replica_groups=mesh['x'=4,'z'=8,'y'=8,'core'=2] {'x','z'}, dimensions={0} | all-to-all | bytes 458752 | tf_op jit(solution)/shard_map/all_to_all | solution.py:308
  148.4 0.7 reduce_sum.12
  (30 shorter events, 1.2 us)
Async XLA Ops:
  0.0 34.2 %copy-start.5 = (s32[2]{0:T(128)S(1)}, s32[2]{0:T(128)}, u32[]{:S(2)}) copy-start(s32[2]{0:T(128)} %param.10) | copy-start | bytes 28
  0.0 39.7 %copy-start.4 = (s32[8,2,32]{2,1,0:T(2,128)S(1)}, s32[8,2,32]{2,1,0:T(2,128)}, u32[]{:S(2)}) copy-start(s32[8,2,32]{2,1,0:T(2,128)} %param.11) | copy-start | bytes 6148
  1.8 24.6 %all-to-all-start = ((bf16[8,224,128]{2,1,0:T(8,128)(2,1)}), bf16[8,224,128]{2,1,0:T(8,128)(2,1)S(1)}, u32[]{:S(2)}, u32[]{:S(2)}) async-start(bf16[8,224,128]{2,1,0:T(8,128)(2,1)} %get-tuple-element.12.many_ref), calls=%async_computation | async-start | bytes 917504 | tf_op jit(solution)/shard_map/all_to_all | solution.py:308
  11.7 10.2 %collective-permute-start.2 = (bf16[80,128]{1,0:T(8,128)(2,1)S(1)}, bf16[80,128]{1,0:T(8,128)(2,1)S(1)}, u32[]{:S(2)}, u32[]{:S(2)}) collective-permute-start(bf16[80,128]{1,0:T(8,128)(2,1)S(1)} %get-tuple-element.13.few_ref), channel_id=1, source_target_pairs={{0,384},{128,0},{256,128},{384,256},{1,385},{129,1},{257,129},{385... | collective-permute-start | bytes 61448 | tf_op jit(solution)/shard_map/ppermute | solution.py:300
  16.4 7.5 %collective-permute-start.1 = (bf16[80,128]{1,0:T(8,128)(2,1)S(1)}, bf16[80,128]{1,0:T(8,128)(2,1)S(1)}, u32[]{:S(2)}, u32[]{:S(2)}) collective-permute-start(bf16[80,128]{1,0:T(8,128)(2,1)S(1)} %get-tuple-element.13.few_ref), channel_id=1, source_target_pairs={{0,256},{128,384},{256,0},{384,128},{1,257},{129,385},{257,1},{385... | collective-permute-start | bytes 61448 | tf_op jit(solution)/shard_map/ppermute | solution.py:300
  19.1 6.9 %collective-permute-start = (bf16[80,128]{1,0:T(8,128)(2,1)S(1)}, bf16[80,128]{1,0:T(8,128)(2,1)S(1)}, u32[]{:S(2)}, u32[]{:S(2)}) collective-permute-start(bf16[80,128]{1,0:T(8,128)(2,1)S(1)} %get-tuple-element.13.few_ref), channel_id=1, source_target_pairs={{0,128},{128,256},{256,384},{384,0},{1,129},{129,257},{257,385},{3... | collective-permute-start | bytes 61448 | tf_op jit(solution)/shard_map/ppermute | solution.py:300
  27.3 24.1 %all-to-all-start.1 = ((bf16[8,4,80,128]{3,2,1,0:T(8,128)(2,1)}), bf16[8,4,80,128]{3,2,1,0:T(8,128)(2,1)S(1)}, u32[]{:S(2)}, u32[]{:S(2)}) async-start(bf16[8,4,80,128]{3,2,1,0:T(8,128)(2,1)} %broadcast_in_dim.32), calls=%async_computation.1 | async-start | bytes 1310720 | tf_op jit(solution)/shard_map/all_to_all | solution.py:308
  34.3 20.8 %collective-permute-start.7 = (bf16[8,224,128]{2,1,0:T(8,128)(2,1)S(1)}, bf16[8,224,128]{2,1,0:T(8,128)(2,1)S(1)}, u32[]{:S(2)}, u32[]{:S(2)}) collective-permute-start(bf16[8,224,128]{2,1,0:T(8,128)(2,1)S(1)} %all-to-all-done.many_ref), channel_id=1, source_target_pairs={{0,256},{128,384},{256,0},{384,128},{1,257},{129,385},{257,1},{385... | collective-permute-start | bytes 1376264 | tf_op jit(solution)/shard_map/ppermute | solution.py:300
  37.7 24.3 %collective-permute-start.3 = (bf16[8,224,128]{2,1,0:T(8,128)(2,1)S(1)}, bf16[8,224,128]{2,1,0:T(8,128)(2,1)S(1)}, u32[]{:S(2)}, u32[]{:S(2)}) collective-permute-start(bf16[8,224,128]{2,1,0:T(8,128)(2,1)S(1)} %all-to-all-done.many_ref), channel_id=1, source_target_pairs={{0,128},{128,256},{256,384},{384,0},{1,129},{129,257},{257,385},{3... | collective-permute-start | bytes 1376264 | tf_op jit(solution)/shard_map/ppermute | solution.py:300
  40.4 26.6 %collective-permute-start.5 = (bf16[8,224,128]{2,1,0:T(8,128)(2,1)S(1)}, bf16[8,224,128]{2,1,0:T(8,128)(2,1)S(1)}, u32[]{:S(2)}, u32[]{:S(2)}) collective-permute-start(bf16[8,224,128]{2,1,0:T(8,128)(2,1)S(1)} %all-to-all-done.many_ref), channel_id=1, source_target_pairs={{0,384},{128,0},{256,128},{384,256},{1,385},{129,1},{257,129},{385... | collective-permute-start | bytes 1376264 | tf_op jit(solution)/shard_map/ppermute | solution.py:300
  51.4 1.7 %copy-start.2 = (bf16[2,1024,576]{1,2,0:T(8,128)(2,1)S(1)}, bf16[2,1024,576]{1,2,0:T(8,128)(2,1)}, u32[]{:S(2)}) copy-start(bf16[2,1024,576]{1,2,0:T(8,128)(2,1)} %param.7) | copy-start | bytes 7077892
  57.1 14.9 %collective-permute-start.8 = (bf16[528,512]{1,0:T(8,128)(2,1)S(1)}, bf16[528,512]{1,0:T(8,128)(2,1)S(1)}, u32[]{:S(2)}, u32[]{:S(2)}) collective-permute-start(bf16[528,512]{1,0:T(8,128)(2,1)S(1)} %local_partial.7), channel_id=1, source_target_pairs={{0,256},{128,384},{256,0},{384,128},{1,257},{129,385},{257,1},{385... | collective-permute-start | bytes 1622024 | tf_op jit(solution)/shard_map/ppermute | solution.py:300
  64.0 21.2 %collective-permute-start.4 = (bf16[528,512]{1,0:T(8,128)(2,1)S(1)}, bf16[528,512]{1,0:T(8,128)(2,1)S(1)}, u32[]{:S(2)}, u32[]{:S(2)}) collective-permute-start(bf16[528,512]{1,0:T(8,128)(2,1)S(1)} %local_partial.5), channel_id=1, source_target_pairs={{0,384},{128,0},{256,128},{384,256},{1,385},{129,1},{257,129},{385... | collective-permute-start | bytes 1622024 | tf_op jit(solution)/shard_map/ppermute | solution.py:300
  69.0 24.1 %copy-start.3 = (bf16[8,2,576]{2,1,0:T(2,128)(2,1)S(1)}, bf16[8,2,576]{2,1,0:T(2,128)(2,1)}, u32[]{:S(2)}) copy-start(bf16[8,2,576]{2,1,0:T(2,128)(2,1)} %param.9) | copy-start | bytes 55300
  69.0 40.5 %copy-start = (bf16[4,512,128]{2,1,0:T(8,128)(2,1)S(1)}, bf16[4,512,128]{2,1,0:T(8,128)(2,1)}, u32[]{:S(2)}) copy-start(bf16[4,512,128]{2,1,0:T(8,128)(2,1)} %up_ref.1) | copy-start | bytes 1572868
  69.1 16.1 %collective-permute-start.6 = (bf16[528,512]{1,0:T(8,128)(2,1)S(1)}, bf16[528,512]{1,0:T(8,128)(2,1)S(1)}, u32[]{:S(2)}, u32[]{:S(2)}) collective-permute-start(bf16[528,512]{1,0:T(8,128)(2,1)S(1)} %local_partial.6), channel_id=1, source_target_pairs={{0,128},{128,256},{256,384},{384,0},{1,129},{129,257},{257,385},{3... | collective-permute-start | bytes 1622024 | tf_op jit(solution)/shard_map/ppermute | solution.py:300
  86.7 41.8 %copy-start.1 = (bf16[512,448]{0,1:T(8,128)(2,1)S(1)}, bf16[512,448]{0,1:T(8,128)(2,1)}, u32[]{:S(2)}) copy-start(bf16[512,448]{0,1:T(8,128)(2,1)} %param.13) | copy-start | bytes 1376260
  86.7 22.8 %all-to-all-start.2 = ((bf16[8,272,128]{2,1,0:T(8,128)(2,1)}), bf16[8,272,128]{2,1,0:T(8,128)(2,1)S(1)}, u32[]{:S(2)}, u32[]{:S(2)}) async-start(bf16[8,272,128]{2,1,0:T(8,128)(2,1)} %combine_x.1), calls=%async_computation.2 | async-start | bytes 1114112 | tf_op jit(solution)/shard_map/all_to_all | solution.py:308

commit v3 on v1

--- a/solution.py
+++ b/solution.py
@@ -77,10 +77,17 @@
     return jnp.concatenate([rope, blank] if r == 0 else [blank, rope], axis=0)
 
 
-def partial_kernel(*refs):
-    q_refs, (keys_ref, bias_ref, out_ref, cols) = refs[:-4], refs[-4:]
-    zs = sum(ref.shape[0] for ref in q_refs)
-    chunk = q_refs[0].shape[1] * 2 // 9
+def cut_for_z(meta, z):
+    tile = meta[:, (z // 2) * 128 : (z // 2 + 1) * 128]
+    if z % 2:
+        tile = pltpu.roll(tile, 64, 1)
+    return tile[:16].astype(jnp.bfloat16)
+
+
+def partial_kernel(for_z, q_ref, keys_ref, bias_ref, out_ref, cols):
+    q_refs = [q_ref]
+    zs = q_ref.shape[0]
+    chunk = q_ref.shape[1] * 2 // 9
     half = chunk // 2
     count = zs * half
     for r in range(2):
@@ -99,18 +106,28 @@
         for z in range(zs):
             at = z * chunk + r * half
             part = slice(z * half, (z + 1) * half)
-            out_ref[at : at + half, :] = summed[part]
             cols[at : at + half, :] = meta[part]
-    end = zs * chunk
-    out_ref[end : end + 16, :] = cols[...].T[:16].astype(jnp.bfloat16)
-
-
-def local_partial(q_chunks, keys, bias):
-    chunk = q_chunks[0].shape[1] * 2 // 9
-    queries = sum(q.shape[0] for q in q_chunks) * chunk
-    return pl.pallas_call(
-        partial_kernel,
-        out_shape=jax.ShapeDtypeStruct((queries + 16, 512), jnp.bfloat16),
+            if not for_z:
+                out_ref[at : at + half, :] = summed[part]
+                continue
+            for k in range(4):
+                to = k * chunk + r * half
+                out_ref[z, to : to + half, :] = summed[part, k * 128 : (k + 1) * 128]
+    meta = cols[...].T
+    if for_z:
+        for z in range(zs):
+            out_ref[z, 4 * chunk :, :] = cut_for_z(meta, z)
+    else:
+        out_ref[zs * chunk :, :] = meta[:16].astype(jnp.bfloat16)
+
+
+def local_partial(q_chunk, keys, bias, for_z=False):
+    zs, chunk = q_chunk.shape[0], q_chunk.shape[1] * 2 // 9
+    queries = zs * chunk
+    shape = (zs, 4 * chunk + 16, 128) if for_z else (queries + 16, 512)
+    return pl.pallas_call(
+        functools.partial(partial_kernel, for_z),
+        out_shape=jax.ShapeDtypeStruct(shape, jnp.bfloat16),
         scratch_shapes=[pltpu.VMEM((queries, 128), jnp.float32)],
         compiler_params=params(32),
         cost_estimate=pl.CostEstimate(
@@ -119,13 +136,13 @@
             transcendentals=queries * keys.shape[2],
         ),
         name="local_partial",
-    )(*q_chunks, keys, bias)
-
-
-def combine_kernel(a_ref, b_ref, c_ref, d_ref, out_ref):
-    refs = (a_ref, b_ref, c_ref, d_ref)
+    )(q_chunk, keys, bias)
+
+
+def combine_kernel(*refs):
+    refs, out_ref = refs[:-1], refs[-1]
     zs = out_ref.shape[0]
-    chunk = (a_ref.shape[0] - 16) // zs
+    chunk = (refs[0].shape[0] - 16) // zs
     count = zs * chunk
     metas = [ref[count : count + 16, :].astype(jnp.float32) for ref in refs]
     tops = [meta[0:1] for meta in metas]
@@ -146,10 +163,7 @@
         ).astype(jnp.bfloat16)
         for k in range(4):
             out_ref[z, k * chunk : (k + 1) * chunk, :] = merged[:, k * 128 : (k + 1) * 128]
-        tile = meta[:, (z // 2) * 128 : (z // 2 + 1) * 128]
-        if z % 2:
-            tile = pltpu.roll(tile, 64, 1)
-        out_ref[z, 4 * chunk : 4 * chunk + 16, :] = tile.astype(jnp.bfloat16)
+        out_ref[z, 4 * chunk :, :] = cut_for_z(meta, z)
 
 
 def combine(parts, zs, chunk):
@@ -204,19 +218,62 @@
     )(packed, fresh, causal)
 
 
-def merge_kernel(got_ref, sum_ref, meta_ref, up_ref, out_ref):
-    zs = got_ref.shape[0]
+def columns(got, count):
+    place = iota((128, 128), 0)
+    stacked = jnp.zeros((128, 128), jnp.float32)
+    for i, read in enumerate(got):
+        meta = read(4 * count, 16).astype(jnp.float32)
+        stacked = jnp.where(place == i, meta[0:1], stacked)
+        stacked = jnp.where(place == len(got) + i, meta[1:2], stacked)
+    cols = stacked.T[:count]
+    return cols[:, : len(got)], cols[:, len(got) : 2 * len(got)]
+
+
+def scaled(got, factors, count, k):
+    return sum(
+        factors[:, i : i + 1] * read(k * count, count).astype(jnp.float32)
+        for i, read in enumerate(got)
+    )
+
+
+def reader(ref, z=None):
+    if z is None:
+        return lambda at, size: ref[at : at + size, :]
+    return lambda at, size: ref[z, at : at + size, :]
+
+
+def gather_kernel(got_ref, out_ref):
+    count = (got_ref.shape[1] - 16) // 4
+    got = [reader(got_ref, z) for z in range(got_ref.shape[0])]
+    tops, totals = columns(got, count)
+    top = jnp.max(tops, axis=1, keepdims=True)
+    factors = jnp.exp(tops - top)
+    total = jnp.sum(factors * totals, axis=1, keepdims=True)
+    for k in range(4):
+        out_ref[k * count : (k + 1) * count, :] = scaled(got, factors, count, k).astype(
+            jnp.bfloat16
+        )
+    lanes = iota((count, 128), 1)
+    meta = jnp.where(lanes == 0, top, jnp.where(lanes == 1, total, 0.0))
+    meta = jnp.concatenate([meta, jnp.zeros((128 - count, 128), jnp.float32)])
+    out_ref[4 * count :, :] = meta.T[:16].astype(jnp.bfloat16)
+
+
+def combine_over_z(got):
+    return pl.pallas_call(
+        gather_kernel,
+        out_shape=jax.ShapeDtypeStruct(got.shape[1:], jnp.bfloat16),
+        compiler_params=params(16),
+        name="combine_z",
+    )(got)
+
+
+def merge_kernel(got_ref, far_ref, sum_ref, meta_ref, up_ref, out_ref):
     count = sum_ref.shape[0]
     heads = up_ref.shape[0]
     rows = count // (heads * STEPS)
-    place = iota((128, 128), 0)
-    stacked = jnp.zeros((128, 128), jnp.float32)
-    for z in range(zs):
-        meta = got_ref[z, 4 * count : 4 * count + 16, :].astype(jnp.float32)
-        stacked = jnp.where(place == z, meta[0:1], stacked)
-        stacked = jnp.where(place == zs + z, meta[1:2], stacked)
-    cols = stacked.T[:count]
-    tops, totals = cols[:, :zs], cols[:, zs : 2 * zs]
+    got = [reader(got_ref, z) for z in range(got_ref.shape[0])] + [reader(far_ref)]
+    tops, totals = columns(got, count)
     own_top, own_total = meta_ref[:, 0:1], meta_ref[:, 1:2]
     top = jnp.maximum(jnp.max(tops, axis=1, keepdims=True), own_top)
     factors = jnp.exp(tops - top)
@@ -225,10 +282,7 @@
     pieces = []
     for k in range(4):
         piece = own_factor * sum_ref[:, k * 128 : (k + 1) * 128]
-        for z in range(zs):
-            block = got_ref[z, k * count : (k + 1) * count, :].astype(jnp.float32)
-            piece = piece + factors[:, z : z + 1] * block
-        pieces.append(piece / bottom)
+        pieces.append((piece + scaled(got, factors, count, k)) / bottom)
     merged = jnp.concatenate(pieces, axis=1)
     for h in range(heads):
         mine = jnp.concatenate(
@@ -239,14 +293,14 @@
             out_ref[copy, :, h * 128 : (h + 1) * 128] = lifted
 
 
-def merge(got, own_sum, own_meta, w_uv, copies):
+def merge(got, far, own_sum, own_meta, w_uv, copies):
     shape = (copies, own_sum.shape[0] // w_uv.shape[0], w_uv.shape[0] * w_uv.shape[2])
     return pl.pallas_call(
         merge_kernel,
         out_shape=jax.ShapeDtypeStruct(shape, jnp.bfloat16),
         compiler_params=params(16),
         name="merge_up",
-    )(got, own_sum, own_meta, w_uv)
+    )(got, far, own_sum, own_meta, w_uv)
 
 
 def project_kernel(rows_ref, w_ref, out_ref):
@@ -288,7 +342,8 @@
     q_rows = jnp.transpose(queries, (1, 2, 0, 3)).reshape(rows * heads * steps, width)
     packed = pack(q_rows, Z_SIZE)
     line = swap_all(packed, "z")
-    far = shift(line, "x", 2, X_SIZE)
+    far = shift(packed[0], "x", 2, X_SIZE)
+    far = swap_all(jnp.broadcast_to(far[None], packed.shape), "z")
     left = shift(line, "x", 1, X_SIZE)
     right = shift(line, "x", -1, X_SIZE)
 
@@ -304,19 +359,19 @@
     fresh = jnp.pad(jnp.transpose(new_latent, (1, 0, 2)), ((0, 0), (0, 128 - steps), (0, 0)))
     own_sum, own_meta = own_part(packed, fresh, causal)
 
-    here = local_partial([line], cache_t, bias)
-    for_left = local_partial([after(left, here)], cache_t, bias)
-    for_right = local_partial([right], cache_t, bias)
-    for_far = local_partial([far], cache_t, bias)
+    here = local_partial(line, cache_t, bias)
+    for_left = local_partial(left, cache_t, bias)
+    for_right = local_partial(right, cache_t, bias)
+    for_far = local_partial(after(far, here), cache_t, bias, for_z=True)
     parts = [
         here,
         shift(for_left, "x", -1, X_SIZE),
         shift(for_right, "x", 1, X_SIZE),
-        shift(for_far, "x", 2, X_SIZE),
     ]
+    home = shift(combine_over_z(swap_all(for_far, "z")), "x", 2, X_SIZE)
     got = swap_all(combine(parts, Z_SIZE, rows * heads * steps), "z")
     groups = lax.axis_size(("y", "core"))
-    attention = swap_all(merge(got, own_sum, own_meta, w_uv, groups), ("y", "core"))
+    attention = swap_all(merge(got, home, own_sum, own_meta, w_uv, groups), ("y", "core"))
     shares = project(attention.reshape(groups * rows * steps, -1), w_out.T)
     shares = shares.reshape(X_SIZE * Z_SIZE, -1, shares.shape[1])
     got_shares = swap_all(shares, ("x", "z"))

time: 147 us -> 151 us (1.027)
  waiting for transfers between devices: 52.9 us -> 38.9 us
  starting transfers between devices: 37.8 us -> 50.4 us
  local copies, waits for them, and re-layouts: 2.83 us -> 8.02 us
    all_to_all x2 -> x4, starting transfers between devices: 14.9 us -> 27.1 us  [swap_all(): return lax.all_to_all(value, axis, split_axis=0, concat_axis=0, tiled=True)]
    all_to_all x2 -> x4, waiting for transfers between devices: 32.1 us -> 22.8 us  [swap_all(): return lax.all_to_all(value, axis, split_axis=0, concat_axis=0, tiled=True)]
    ppermute x6, waiting for transfers between devices: 20.8 us -> 16.1 us  [shift(): lax.ppermute(value, axis, [(i, (i + by) % size) for i in range(size)])]
    unnamed x9 -> x17, local copies, waits for them, and re-layouts: 1.68 us -> 5.02 us
    pallas_call x4 -> x5, Pallas kernels: 7.85 us -> 9.21 us  [the longest x4 8.68 us: local_partial(): pl.pallas_call(functools.partial(partial_kernel, for_z), out_shape=jax.Sh...]
  transfers between devices with their start and end apart: 8 -> 10, of which waited for: 6 -> 7; matrix products, arithmetic and copies ran while one was open for 1% -> 1% of each run, Pallas kernels for 6% -> 8%
where the time goes in v3:
time: 151 us; the launch traced here: 150 us
  starting transfers between devices  50.4 us (33%)
  waiting for transfers between devices  38.9 us (26%)
  blocking collectives  37.2 us (25%)
  Pallas kernels  14.3 us (9%)
  local copies, waits for them, and re-layouts  8.02 us (5%)
    all_to_all x2, blocking collectives, swap_all(): return lax.all_to_all(value, axis, split_axis=0, concat_axis=0, tiled=True)  37.2 us
    all_to_all x4, starting transfers between devices, swap_all(): return lax.all_to_all(value, axis, split_axis=0, concat_axis=0, tiled=True)  27.1 us
    ppermute x6, starting transfers between devices, shift(): lax.ppermute(value, axis, [(i, (i + by) % size) for i in range(size)])  23.3 us
    all_to_all x4, waiting for transfers between devices, swap_all(): return lax.all_to_all(value, axis, split_axis=0, concat_axis=0, tiled=True)  22.8 us
    ppermute x6, waiting for transfers between devices, shift(): lax.ppermute(value, axis, [(i, (i + by) % size) for i in range(size)])  16.1 us
    pallas_call x4, Pallas kernels, local_partial(): pl.pallas_call(functools.partial(partial_kernel, for_z), out_shape=jax.Sh...  8.68 us
    unnamed x17, local copies, waits for them, and re-layouts  5.02 us
  transfers between devices with their start and end apart: 10, of which 7 were waited for; matrix products, arithmetic and copies ran while one was open for 1% of the time, Pallas kernels for 8%

profile of v3, /device:TPU:64, one launch (start us, length us, event | category | flops | bytes accessed | tf_op | source)
XLA Modules:
  0.0 150.2 jit_solution(16057432085108794519)
XLA Ops:
  0.0 0.9 copy.10
  0.9 0.9 pack_queries.1.q_ref
  1.8 10.0 %all-to-all-start = ((bf16[8,288,128]{2,1,0:T(8,128)(2,1)}), bf16[8,288,128]{2,1,0:T(8,128)(2,1)S(1)}, u32[]{:S(2)}, u32[]{:S(2)}) async-start(bf16[8,288,128]{2,1,0:T(8,128)(2,1)} %pack_queries.1.q_ref), calls=%async_computation | async-start | bytes 1179648 | tf_op jit(solution)/shard_map/all_to_all | solution.py:334
  11.8 0.9 slice_bitcast_fusion
  12.7 4.9 %collective-permute-start.4 = (bf16[288,128]{1,0:T(8,128)(2,1)S(1)}, bf16[288,128]{1,0:T(8,128)(2,1)S(1)}, u32[]{:S(2)}, u32[]{:S(2)}) collective-permute-start(bf16[288,128]{1,0:T(8,128)(2,1)S(1)} %slice_bitcast_fusion), channel_id=1, source_target_pairs={{0,256},{128,384},{256,0},{384,128},{1,257},{129,385},{257,1},{385... | collective-permute-start | bytes 221192 | tf_op jit(solution)/shard_map/ppermute | solution.py:326
  17.7 2.8 %collective-permute-done.4 = bf16[288,128]{1,0:T(8,128)(2,1)S(1)} collective-permute-done((bf16[288,128]{1,0:T(8,128)(2,1)S(1)}, bf16[288,128]{1,0:T(8,128)(2,1)S(1)}, u32[]{:S(2)}, u32[]{:S(2)}) %collective-permute-start.4) | collective-permute-done | bytes 73760 | tf_op jit(solution)/shard_map/ppermute | solution.py:326
  20.5 8.8 %all-to-all-done.q_ref = bf16[8,288,128]{2,1,0:T(8,128)(2,1)S(1)} async-done(((bf16[8,288,128]{2,1,0:T(8,128)(2,1)}), bf16[8,288,128]{2,1,0:T(8,128)(2,1)S(1)}, u32[]{:S(2)}, u32[]{:S(2)}) %all-to-all-start) | async-done | bytes 589856 | tf_op jit(solution)/shard_map/all_to_all | solution.py:334
  29.2 0.9 broadcast_in_dim.35
  30.1 4.9 %all-to-all-start.2 = ((bf16[8,288,128]{2,1,0:T(8,128)(2,1)}), bf16[8,288,128]{2,1,0:T(8,128)(2,1)S(1)}, u32[]{:S(2)}, u32[]{:S(2)}) async-start(bf16[8,288,128]{2,1,0:T(8,128)(2,1)} %broadcast_in_dim.35), calls=%async_computation.2 | async-start | bytes 1179648 | tf_op jit(solution)/shard_map/all_to_all | solution.py:334
  35.8 4.7 %collective-permute-start.2 = (bf16[8,288,128]{2,1,0:T(8,128)(2,1)S(1)}, bf16[8,288,128]{2,1,0:T(8,128)(2,1)S(1)}, u32[]{:S(2)}, u32[]{:S(2)}) collective-permute-start(bf16[8,288,128]{2,1,0:T(8,128)(2,1)S(1)} %all-to-all-done.q_ref), channel_id=1, source_target_pairs={{0,384},{128,0},{256,128},{384,256},{1,385},{129,1},{257,129},{385... | collective-permute-start | bytes 1769480 | tf_op jit(solution)/shard_map/ppermute | solution.py:326
  40.5 1.9 %collective-permute-start = (bf16[8,288,128]{2,1,0:T(8,128)(2,1)S(1)}, bf16[8,288,128]{2,1,0:T(8,128)(2,1)S(1)}, u32[]{:S(2)}, u32[]{:S(2)}) collective-permute-start(bf16[8,288,128]{2,1,0:T(8,128)(2,1)S(1)} %all-to-all-done.q_ref), channel_id=1, source_target_pairs={{0,128},{128,256},{256,384},{384,0},{1,129},{129,257},{257,385},{3... | collective-permute-start | bytes 1769480 | tf_op jit(solution)/shard_map/ppermute | solution.py:326
  42.5 1.7 %copy-done.2 = bf16[2,1024,576]{1,2,0:T(8,128)(2,1)S(1)} copy-done((bf16[2,1024,576]{1,2,0:T(8,128)(2,1)S(1)}, bf16[2,1024,576]{1,2,0:T(8,128)(2,1)}, u32[]{:S(2)}) %copy-start.2) | copy-done | bytes 2359320
  44.1 2.0 %local_partial.4.refs_0_ = bf16[528,512]{1,0:T(8,128)(2,1)S(1)} custom-call(bf16[8,288,128]{2,1,0:T(8,128)(2,1)S(1)} %all-to-all-done.q_ref, bf16[2,576,1024]{2,1,0:T(8,128)(2,1)S(1)} %bitcast.21, f32[2,8,1024]{2,1,0:T(8,128)S(1)} %select_bitcast_fusion.bias_ref), custom_call_target="tpu_custom_call" | custom-call | flops 1207959552 | bytes 4194304 | tf_op jit(solution)/shard_map/local_partial/pallas_call | solution.py:128
  46.1 6.9 %all-to-all-done.2.q_ref = bf16[8,288,128]{2,1,0:T(8,128)(2,1)S(1)} async-done(((bf16[8,288,128]{2,1,0:T(8,128)(2,1)}), bf16[8,288,128]{2,1,0:T(8,128)(2,1)S(1)}, u32[]{:S(2)}, u32[]{:S(2)}) %all-to-all-start.2) | async-done | bytes 589856 | tf_op jit(solution)/shard_map/all_to_all | solution.py:334
  53.0 1.7 %copy-done.3 = bf16[2,1024,576]{1,2,0:T(8,128)(2,1)S(1)} copy-done((bf16[2,1024,576]{1,2,0:T(8,128)(2,1)S(1)}, bf16[2,1024,576]{1,2,0:T(8,128)(2,1)}, u32[]{:S(2)}) %copy-start.3) | copy-done | bytes 2359320
  54.6 2.8 %local_partial.7 = bf16[8,272,128]{2,1,0:T(8,128)(2,1)} custom-call(bf16[8,288,128]{2,1,0:T(8,128)(2,1)S(1)} %all-to-all-done.2.q_ref, bf16[2,576,1024]{2,1,0:T(8,128)(2,1)S(1)} %bitcast.22, f32[2,8,1024]{2,1,0:T(8,128)S(1)} %select_bitcast_fusion.bias_ref), custom_call_target="tpu_custom_call" | custom-call | flops 1207959552 | bytes 4194304 | tf_op jit(solution)/shard_map/local_partial/pallas_call | solution.py:128
  57.4 4.9 %all-to-all-start.3 = ((bf16[8,272,128]{2,1,0:T(8,128)(2,1)}), bf16[8,272,128]{2,1,0:T(8,128)(2,1)S(1)}, u32[]{:S(2)}, u32[]{:S(2)}) async-start(bf16[8,272,128]{2,1,0:T(8,128)(2,1)} %local_partial.7), calls=%async_computation.3 | async-start | bytes 1114112 | tf_op jit(solution)/shard_map/all_to_all | solution.py:334
  62.3 1.7 %copy-done.4 = bf16[2,1024,576]{1,2,0:T(8,128)(2,1)S(1)} copy-done((bf16[2,1024,576]{1,2,0:T(8,128)(2,1)S(1)}, bf16[2,1024,576]{1,2,0:T(8,128)(2,1)}, u32[]{:S(2)}) %copy-start.4) | copy-done | bytes 2359320
  64.0 2.0 %local_partial.6 = bf16[528,512]{1,0:T(8,128)(2,1)S(1)} custom-call(bf16[8,288,128]{2,1,0:T(8,128)(2,1)S(1)} %collective-permute-done.2.q_ref, bf16[2,576,1024]{2,1,0:T(8,128)(2,1)S(1)} %bitcast.23, f32[2,8,1024]{2,1,0:T(8,128)S(1)} %select_bitcast_fusion.bias_ref), custom_call_target="tpu_custom_call" | custom-call | flops 1207959552 | bytes 4194304 | tf_op jit(solution)/shard_map/local_partial/pallas_call | solution.py:128
  66.0 3.4 %collective-permute-start.3 = (bf16[528,512]{1,0:T(8,128)(2,1)S(1)}, bf16[528,512]{1,0:T(8,128)(2,1)S(1)}, u32[]{:S(2)}, u32[]{:S(2)}) collective-permute-start(bf16[528,512]{1,0:T(8,128)(2,1)S(1)} %local_partial.6), channel_id=1, source_target_pairs={{0,128},{128,256},{256,384},{384,0},{1,129},{129,257},{257,385},{3... | collective-permute-start | bytes 1622024 | tf_op jit(solution)/shard_map/ppermute | solution.py:326
  69.4 2.0 %local_partial.5 = bf16[528,512]{1,0:T(8,128)(2,1)S(1)} custom-call(bf16[8,288,128]{2,1,0:T(8,128)(2,1)S(1)} %collective-permute-done.q_ref, bf16[2,576,1024]{2,1,0:T(8,128)(2,1)S(1)} %bitcast.24, f32[2,8,1024]{2,1,0:T(8,128)S(1)} %select_bitcast_fusion.bias_ref), custom_call_target="tpu_custom_call" | custom-call | flops 1207959552 | bytes 4194304 | tf_op jit(solution)/shard_map/local_partial/pallas_call | solution.py:128
  71.4 3.8 %collective-permute-start.1 = (bf16[528,512]{1,0:T(8,128)(2,1)S(1)}, bf16[528,512]{1,0:T(8,128)(2,1)S(1)}, u32[]{:S(2)}, u32[]{:S(2)}) collective-permute-start(bf16[528,512]{1,0:T(8,128)(2,1)S(1)} %local_partial.5), channel_id=1, source_target_pairs={{0,384},{128,0},{256,128},{384,256},{1,385},{129,1},{257,129},{385... | collective-permute-start | bytes 1622024 | tf_op jit(solution)/shard_map/ppermute | solution.py:326
  75.2 7.8 %collective-permute-done.3.refs_2_ = bf16[528,512]{1,0:T(8,128)(2,1)S(1)} collective-permute-done((bf16[528,512]{1,0:T(8,128)(2,1)S(1)}, bf16[528,512]{1,0:T(8,128)(2,1)S(1)}, u32[]{:S(2)}, u32[]{:S(2)}) %collective-permute-start.3) | collective-permute-done | bytes 540704 | tf_op jit(solution)/shard_map/ppermute | solution.py:326
  83.0 4.1 %collective-permute-done.1.refs_1_ = bf16[528,512]{1,0:T(8,128)(2,1)S(1)} collective-permute-done((bf16[528,512]{1,0:T(8,128)(2,1)S(1)}, bf16[528,512]{1,0:T(8,128)(2,1)S(1)}, u32[]{:S(2)}, u32[]{:S(2)}) %collective-permute-start.1) | collective-permute-done | bytes 540704 | tf_op jit(solution)/shard_map/ppermute | solution.py:326
  87.1 1.3 combine_x.1
  88.4 7.3 %all-to-all-start.1 = ((bf16[8,272,128]{2,1,0:T(8,128)(2,1)}), bf16[8,272,128]{2,1,0:T(8,128)(2,1)S(1)}, u32[]{:S(2)}, u32[]{:S(2)}) async-start(bf16[8,272,128]{2,1,0:T(8,128)(2,1)} %combine_x.1), calls=%async_computation.1 | async-start | bytes 1114112 | tf_op jit(solution)/shard_map/all_to_all | solution.py:334
  96.3 4.6 %collective-permute-start.5 = (bf16[272,128]{1,0:T(8,128)(2,1)S(1)}, bf16[272,128]{1,0:T(8,128)(2,1)S(1)}, u32[]{:S(2)}, u32[]{:S(2)}) collective-permute-start(bf16[272,128]{1,0:T(8,128)(2,1)S(1)} %combine_z.1), channel_id=1, source_target_pairs={{0,256},{128,384},{256,0},{384,128},{1,257},{129,385},{257,1},{385... | collective-permute-start | bytes 208904 | tf_op jit(solution)/shard_map/ppermute | solution.py:326
  101.0 1.6 %own_part.1 = (f32[64,512]{1,0:T(8,128)S(1)}, f32[64,128]{1,0:T(8,128)S(1)}) custom-call(bf16[8,288,128]{2,1,0:T(8,128)(2,1)} %pack_queries.1.q_ref, bf16[2,128,576]{2,1,0:T(8,128)(2,1)S(1)} %pad.4.fresh_ref, f32[8,128]{1,0:T(8,128)S(1)} %fusion.bias_ref), custom_call_target="tpu_custom_call" | custom-call | tf_op jit(solution)/shard_map/own_part/pallas_call | solution.py:200
  102.6 1.4 collective-permute-done.5.far_ref
  104.0 7.2 %all-to-all-done.1.got_ref = bf16[8,272,128]{2,1,0:T(8,128)(2,1)S(1)} async-done(((bf16[8,272,128]{2,1,0:T(8,128)(2,1)}), bf16[8,272,128]{2,1,0:T(8,128)(2,1)S(1)}, u32[]{:S(2)}, u32[]{:S(2)}) %all-to-all-start.1) | async-done | bytes 557088 | tf_op jit(solution)/shard_map/all_to_all | solution.py:334
  112.0 18.2 %all_to_all.30 = bf16[16,16,512]{2,1,0:T(8,128)(2,1)S(1)} all-to-all(bf16[16,16,512]{2,1,0:T(8,128)(2,1)S(1)} %merge_up.1), channel_id=1, replica_groups=mesh['x'=4,'z'=8,'y'=8,'core'=2] {'y','core'}, dimensions={0} | all-to-all | bytes 524288 | tf_op jit(solution)/shard_map/all_to_all | solution.py:334
  130.6 19.0 %all_to_all.31 = bf16[32,8,448]{2,1,0:T(8,128)(2,1)S(1)} all-to-all(bf16[32,8,448]{2,1,0:T(8,128)(2,1)S(1)} %bitcast.18), channel_id=1, replica_groups=mesh['x'=4,'z'=8,'y'=8,'core'=2] {'x','z'}, dimensions={0} | all-to-all | bytes 458752 | tf_op jit(solution)/shard_map/all_to_all | solution.py:334
  (31 shorter events, 3.2 us)
Async XLA Ops:
  0.0 35.0 %copy-start.6 = (s32[8,2,32]{2,1,0:T(2,128)S(1)}, s32[8,2,32]{2,1,0:T(2,128)}, u32[]{:S(2)}) copy-start(s32[8,2,32]{2,1,0:T(2,128)} %param.11) | copy-start | bytes 6148
  0.0 35.7 %copy-start.7 = (s32[2]{0:T(128)S(1)}, s32[2]{0:T(128)}, u32[]{:S(2)}) copy-start(s32[2]{0:T(128)} %param.10) | copy-start | bytes 28
  1.8 27.4 %all-to-all-start = ((bf16[8,288,128]{2,1,0:T(8,128)(2,1)}), bf16[8,288,128]{2,1,0:T(8,128)(2,1)S(1)}, u32[]{:S(2)}, u32[]{:S(2)}) async-start(bf16[8,288,128]{2,1,0:T(8,128)(2,1)} %pack_queries.1.q_ref), calls=%async_computation | async-start | bytes 1179648 | tf_op jit(solution)/shard_map/all_to_all | solution.py:334
  12.7 7.7 %collective-permute-start.4 = (bf16[288,128]{1,0:T(8,128)(2,1)S(1)}, bf16[288,128]{1,0:T(8,128)(2,1)S(1)}, u32[]{:S(2)}, u32[]{:S(2)}) collective-permute-start(bf16[288,128]{1,0:T(8,128)(2,1)S(1)} %slice_bitcast_fusion), channel_id=1, source_target_pairs={{0,256},{128,384},{256,0},{384,128},{1,257},{129,385},{257,1},{385... | collective-permute-start | bytes 221192 | tf_op jit(solution)/shard_map/ppermute | solution.py:326
  30.1 22.8 %all-to-all-start.2 = ((bf16[8,288,128]{2,1,0:T(8,128)(2,1)}), bf16[8,288,128]{2,1,0:T(8,128)(2,1)S(1)}, u32[]{:S(2)}, u32[]{:S(2)}) async-start(bf16[8,288,128]{2,1,0:T(8,128)(2,1)} %broadcast_in_dim.35), calls=%async_computation.2 | async-start | bytes 1179648 | tf_op jit(solution)/shard_map/all_to_all | solution.py:334
  35.8 26.5 %collective-permute-start.2 = (bf16[8,288,128]{2,1,0:T(8,128)(2,1)S(1)}, bf16[8,288,128]{2,1,0:T(8,128)(2,1)S(1)}, u32[]{:S(2)}, u32[]{:S(2)}) collective-permute-start(bf16[8,288,128]{2,1,0:T(8,128)(2,1)S(1)} %all-to-all-done.q_ref), channel_id=1, source_target_pairs={{0,384},{128,0},{256,128},{384,256},{1,385},{129,1},{257,129},{385... | collective-permute-start | bytes 1769480 | tf_op jit(solution)/shard_map/ppermute | solution.py:326
  40.5 28.9 %collective-permute-start = (bf16[8,288,128]{2,1,0:T(8,128)(2,1)S(1)}, bf16[8,288,128]{2,1,0:T(8,128)(2,1)S(1)}, u32[]{:S(2)}, u32[]{:S(2)}) collective-permute-start(bf16[8,288,128]{2,1,0:T(8,128)(2,1)S(1)} %all-to-all-done.q_ref), channel_id=1, source_target_pairs={{0,128},{128,256},{256,384},{384,0},{1,129},{129,257},{257,385},{3... | collective-permute-start | bytes 1769480 | tf_op jit(solution)/shard_map/ppermute | solution.py:326
  42.4 1.7 %copy-start.2 = (bf16[2,1024,576]{1,2,0:T(8,128)(2,1)S(1)}, bf16[2,1024,576]{1,2,0:T(8,128)(2,1)}, u32[]{:S(2)}) copy-start(bf16[2,1024,576]{1,2,0:T(8,128)(2,1)} %param.7) | copy-start | bytes 7077892
  53.0 1.7 %copy-start.3 = (bf16[2,1024,576]{1,2,0:T(8,128)(2,1)S(1)}, bf16[2,1024,576]{1,2,0:T(8,128)(2,1)}, u32[]{:S(2)}) copy-start(bf16[2,1024,576]{1,2,0:T(8,128)(2,1)} %param.7) | copy-start | bytes 7077892
  57.4 31.0 %all-to-all-start.3 = ((bf16[8,272,128]{2,1,0:T(8,128)(2,1)}), bf16[8,272,128]{2,1,0:T(8,128)(2,1)S(1)}, u32[]{:S(2)}, u32[]{:S(2)}) async-start(bf16[8,272,128]{2,1,0:T(8,128)(2,1)} %local_partial.7), calls=%async_computation.3 | async-start | bytes 1114112 | tf_op jit(solution)/shard_map/all_to_all | solution.py:334
  62.3 1.7 %copy-start.4 = (bf16[2,1024,576]{1,2,0:T(8,128)(2,1)S(1)}, bf16[2,1024,576]{1,2,0:T(8,128)(2,1)}, u32[]{:S(2)}) copy-start(bf16[2,1024,576]{1,2,0:T(8,128)(2,1)} %param.7) | copy-start | bytes 7077892
  66.0 17.0 %collective-permute-start.3 = (bf16[528,512]{1,0:T(8,128)(2,1)S(1)}, bf16[528,512]{1,0:T(8,128)(2,1)S(1)}, u32[]{:S(2)}, u32[]{:S(2)}) collective-permute-start(bf16[528,512]{1,0:T(8,128)(2,1)S(1)} %local_partial.6), channel_id=1, source_target_pairs={{0,128},{128,256},{256,384},{384,0},{1,129},{129,257},{257,385},{3... | collective-permute-start | bytes 1622024 | tf_op jit(solution)/shard_map/ppermute | solution.py:326
  71.4 24.4 %copy-start.5 = (bf16[8,2,576]{2,1,0:T(2,128)(2,1)S(1)}, bf16[8,2,576]{2,1,0:T(2,128)(2,1)}, u32[]{:S(2)}) copy-start(bf16[8,2,576]{2,1,0:T(2,128)(2,1)} %param.9) | copy-start | bytes 55300
  71.4 39.8 %copy-start = (bf16[4,512,128]{2,1,0:T(8,128)(2,1)S(1)}, bf16[4,512,128]{2,1,0:T(8,128)(2,1)}, u32[]{:S(2)}) copy-start(bf16[4,512,128]{2,1,0:T(8,128)(2,1)} %up_ref.1) | copy-start | bytes 1572868
  71.4 15.7 %collective-permute-start.1 = (bf16[528,512]{1,0:T(8,128)(2,1)S(1)}, bf16[528,512]{1,0:T(8,128)(2,1)S(1)}, u32[]{:S(2)}, u32[]{:S(2)}) collective-permute-start(bf16[528,512]{1,0:T(8,128)(2,1)S(1)} %local_partial.5), channel_id=1, source_target_pairs={{0,384},{128,0},{256,128},{384,256},{1,385},{129,1},{257,129},{385... | collective-permute-start | bytes 1622024 | tf_op jit(solution)/shard_map/ppermute | solution.py:326
  88.4 41.7 %copy-start.1 = (bf16[512,448]{0,1:T(8,128)(2,1)S(1)}, bf16[512,448]{0,1:T(8,128)(2,1)}, u32[]{:S(2)}) copy-start(bf16[512,448]{0,1:T(8,128)(2,1)} %param.13) | copy-start | bytes 1376260
  88.4 22.8 %all-to-all-start.1 = ((bf16[8,272,128]{2,1,0:T(8,128)(2,1)}), bf16[8,272,128]{2,1,0:T(8,128)(2,1)S(1)}, u32[]{:S(2)}, u32[]{:S(2)}) async-start(bf16[8,272,128]{2,1,0:T(8,128)(2,1)} %combine_x.1), calls=%async_computation.1 | async-start | bytes 1114112 | tf_op jit(solution)/shard_map/all_to_all | solution.py:334
  96.3 7.7 %collective-permute-start.5 = (bf16[272,128]{1,0:T(8,128)(2,1)S(1)}, bf16[272,128]{1,0:T(8,128)(2,1)S(1)}, u32[]{:S(2)}, u32[]{:S(2)}) collective-permute-start(bf16[272,128]{1,0:T(8,128)(2,1)S(1)} %combine_z.1), channel_id=1, source_target_pairs={{0,256},{128,384},{256,0},{384,128},{1,257},{129,385},{257,1},{385... | collective-permute-start | bytes 208904 | tf_op jit(solution)/shard_map/ppermute | solution.py:326

commit v4 on v1

--- a/solution.py
+++ b/solution.py
@@ -35,17 +35,23 @@
     return lax.broadcasted_iota(jnp.int32, shape, axis)
 
 
-def pack_kernel(q_ref, out_ref):
+def pack_kernel(q_ref, out_ref, packed, sems):
     count = q_ref.shape[0]
     half = count // 2
     blocks = [q_ref[:, k * 128 : (k + 1) * 128] for k in range(4)]
     rope = q_ref[:, 512:576].astype(jnp.float32)
     wide = jnp.concatenate([rope, rope], axis=1)
     rope = jnp.where(iota((half, 128), 1) < 64, wide[:half], wide[half:]).astype(jnp.bfloat16)
-    for z in range(out_ref.shape[0]):
-        for k in range(4):
-            out_ref[z, k * count : (k + 1) * count, :] = blocks[k]
-        out_ref[z, 4 * count :, :] = rope
+    for k in range(4):
+        packed[k * count : (k + 1) * count, :] = blocks[k]
+    packed[4 * count :, :] = rope
+    copies = [
+        pltpu.make_async_copy(packed, out_ref.at[z], sems.at[z]) for z in range(out_ref.shape[0])
+    ]
+    for copy in copies:
+        copy.start()
+    for copy in copies:
+        copy.wait()
 
 
 def pack(q_rows, copies):
@@ -53,6 +59,11 @@
     return pl.pallas_call(
         pack_kernel,
         out_shape=jax.ShapeDtypeStruct((copies, 4 * count + count // 2, 128), jnp.bfloat16),
+        out_specs=pl.BlockSpec(memory_space=pl.ANY),
+        scratch_shapes=[
+            pltpu.VMEM((4 * count + count // 2, 128), jnp.bfloat16),
+            pltpu.SemaphoreType.DMA((copies,)),
+        ],
         compiler_params=params(8),
         name="pack_queries",
     )(q_rows)
@@ -122,7 +133,7 @@
     )(*q_chunks, keys, bias)
 
 
-def combine_kernel(a_ref, b_ref, c_ref, d_ref, out_ref):
+def combine_kernel(a_ref, b_ref, c_ref, d_ref, out_ref, pieces, sems):
     refs = (a_ref, b_ref, c_ref, d_ref)
     zs = out_ref.shape[0]
     chunk = (a_ref.shape[0] - 16) // zs
@@ -139,23 +150,32 @@
     cols = stacked.T
     place = iota((16, count), 0)
     meta = jnp.where(place == 0, top, jnp.where(place == 1, total, 0.0))
+    copies = [pltpu.make_async_copy(pieces.at[z], out_ref.at[z], sems.at[z]) for z in range(zs)]
     for z in range(zs):
         rows = slice(z * chunk, (z + 1) * chunk)
         merged = sum(
             cols[rows, i : i + 1] * ref[rows, :].astype(jnp.float32) for i, ref in enumerate(refs)
         ).astype(jnp.bfloat16)
         for k in range(4):
-            out_ref[z, k * chunk : (k + 1) * chunk, :] = merged[:, k * 128 : (k + 1) * 128]
+            pieces[z, k * chunk : (k + 1) * chunk, :] = merged[:, k * 128 : (k + 1) * 128]
         tile = meta[:, (z // 2) * 128 : (z // 2 + 1) * 128]
         if z % 2:
             tile = pltpu.roll(tile, 64, 1)
-        out_ref[z, 4 * chunk : 4 * chunk + 16, :] = tile.astype(jnp.bfloat16)
+        pieces[z, 4 * chunk : 4 * chunk + 16, :] = tile.astype(jnp.bfloat16)
+        copies[z].start()
+    for copy in copies:
+        copy.wait()
 
 
 def combine(parts, zs, chunk):
     return pl.pallas_call(
         combine_kernel,
         out_shape=jax.ShapeDtypeStruct((zs, 4 * chunk + 16, 128), jnp.bfloat16),
+        out_specs=pl.BlockSpec(memory_space=pl.ANY),
+        scratch_shapes=[
+            pltpu.VMEM((zs, 4 * chunk + 16, 128), jnp.bfloat16),
+            pltpu.SemaphoreType.DMA((zs,)),
+        ],
         compiler_params=params(16),
         name="combine_x",
     )(*parts)
@@ -287,16 +307,18 @@
 
     q_rows = jnp.transpose(queries, (1, 2, 0, 3)).reshape(rows * heads * steps, width)
     packed = pack(q_rows, Z_SIZE)
-    line = swap_all(packed, "z")
-    far = shift(line, "x", 2, X_SIZE)
-    left = shift(line, "x", 1, X_SIZE)
-    right = shift(line, "x", -1, X_SIZE)
-
+
+    selection, lengths = after((selection, lengths), packed)
     blocks = shard * (keys // BLOCK) + jnp.arange(keys // BLOCK, dtype=jnp.int32)
     chosen = jnp.any(selection[:, :, :, None] == blocks, axis=2)
     positions = shard * keys + jnp.arange(keys, dtype=jnp.int32)
     live = jnp.repeat(chosen, BLOCK, axis=2) & (positions < lengths[:, None])[None]
     bias = jnp.where(jnp.transpose(live, (1, 0, 2)), 0.0, DEAD)
+    line = after(swap_all(packed, "z"), bias)
+    far = shift(line, "x", 2, X_SIZE)
+    left = shift(line, "x", 1, X_SIZE)
+    right = shift(line, "x", -1, X_SIZE)
+
     cache_t = jnp.transpose(latent_cache, (0, 2, 1))
 
     ids = jnp.arange(128, dtype=jnp.int32)

time: 147 us -> 147 us (level)
    all_to_all x2, waiting for transfers between devices: 32.1 us -> 30 us  [swap_all(): return lax.all_to_all(value, axis, split_axis=0, concat_axis=0, tiled=True)]
    ppermute x6, waiting for transfers between devices: 20.8 us -> 22.9 us  [shift(): lax.ppermute(value, axis, [(i, (i + by) % size) for i in range(size)])]
where the time goes in v4:
time: 147 us; the launch traced here: 146 us
  waiting for transfers between devices  52.9 us (36%)
  starting transfers between devices  37.9 us (26%)
  blocking collectives  37.2 us (25%)
  Pallas kernels  13 us (9%)
  local copies, waits for them, and re-layouts  2.84 us (2%)
  other arithmetic  2.53 us (2%)
    all_to_all x2, blocking collectives, swap_all(): return lax.all_to_all(value, axis, split_axis=0, concat_axis=0, tiled=True)  37.2 us
    all_to_all x2, waiting for transfers between devices, swap_all(): return lax.all_to_all(value, axis, split_axis=0, concat_axis=0, tiled=True)  30 us
    ppermute x6, starting transfers between devices, shift(): lax.ppermute(value, axis, [(i, (i + by) % size) for i in range(size)])  22.9 us
    ppermute x6, waiting for transfers between devices, shift(): lax.ppermute(value, axis, [(i, (i + by) % size) for i in range(size)])  22.9 us
    all_to_all x2, starting transfers between devices, swap_all(): return lax.all_to_all(value, axis, split_axis=0, concat_axis=0, tiled=True)  15 us
    pallas_call x4, Pallas kernels, local_partial(): pl.pallas_call(partial_kernel, out_shape=jax.ShapeDtypeStruct((queries +...  7.87 us
  transfers between devices with their start and end apart: 8, of which 6 were waited for; matrix products, arithmetic and copies ran while one was open for 1% of the time, Pallas kernels for 6%

profile of v4, /device:TPU:64, one launch (start us, length us, event | category | flops | bytes accessed | tf_op | source)
XLA Modules:
  0.0 146.5 jit_solution(5548842946141755474)
XLA Ops:
  0.0 0.9 copy.10
  0.9 1.0 pack_queries.1.q_ref
  1.9 10.0 %all-to-all-start = ((bf16[8,288,128]{2,1,0:T(8,128)(2,1)}), bf16[8,288,128]{2,1,0:T(8,128)(2,1)S(1)}, u32[]{:S(2)}, u32[]{:S(2)}) async-start(bf16[8,288,128]{2,1,0:T(8,128)(2,1)} %pack_queries.1.q_ref), calls=%async_computation | async-start | bytes 1179648 | tf_op jit(solution)/shard_map/all_to_all | solution.py:300
  11.9 1.1 compare_reduce_fusion
  13.0 0.1 broadcast_in_dim.26
  13.1 0.1 reshape.48
  13.2 0.7 broadcast_compare_fusion
  14.0 15.3 %all-to-all-done.refs_0_ = bf16[8,288,128]{2,1,0:T(8,128)(2,1)S(1)} async-done(((bf16[8,288,128]{2,1,0:T(8,128)(2,1)}), bf16[8,288,128]{2,1,0:T(8,128)(2,1)S(1)}, u32[]{:S(2)}, u32[]{:S(2)}) %all-to-all-start) | async-done | bytes 589856 | tf_op jit(solution)/shard_map/all_to_all | solution.py:300
  29.3 4.9 %collective-permute-start.4 = (bf16[8,288,128]{2,1,0:T(8,128)(2,1)S(1)}, bf16[8,288,128]{2,1,0:T(8,128)(2,1)S(1)}, u32[]{:S(2)}, u32[]{:S(2)}) collective-permute-start(bf16[8,288,128]{2,1,0:T(8,128)(2,1)S(1)} %all-to-all-done.refs_0_), channel_id=1, source_target_pairs={{0,256},{128,384},{256,0},{384,128},{1,257},{129,385},{257,1},{385... | collective-permute-start | bytes 1769480 | tf_op jit(solution)/shard_map/ppermute | solution.py:292
  34.2 3.0 %collective-permute-start.2 = (bf16[8,288,128]{2,1,0:T(8,128)(2,1)S(1)}, bf16[8,288,128]{2,1,0:T(8,128)(2,1)S(1)}, u32[]{:S(2)}, u32[]{:S(2)}) collective-permute-start(bf16[8,288,128]{2,1,0:T(8,128)(2,1)S(1)} %all-to-all-done.refs_0_), channel_id=1, source_target_pairs={{0,384},{128,0},{256,128},{384,256},{1,385},{129,1},{257,129},{385... | collective-permute-start | bytes 1769480 | tf_op jit(solution)/shard_map/ppermute | solution.py:292
  37.3 2.8 %collective-permute-start = (bf16[8,288,128]{2,1,0:T(8,128)(2,1)S(1)}, bf16[8,288,128]{2,1,0:T(8,128)(2,1)S(1)}, u32[]{:S(2)}, u32[]{:S(2)}) collective-permute-start(bf16[8,288,128]{2,1,0:T(8,128)(2,1)S(1)} %all-to-all-done.refs_0_), channel_id=1, source_target_pairs={{0,128},{128,256},{256,384},{384,0},{1,129},{129,257},{257,385},{3... | collective-permute-start | bytes 1769480 | tf_op jit(solution)/shard_map/ppermute | solution.py:292
  40.1 1.7 %copy-done.2 = bf16[2,1024,576]{1,2,0:T(8,128)(2,1)S(1)} copy-done((bf16[2,1024,576]{1,2,0:T(8,128)(2,1)S(1)}, bf16[2,1024,576]{1,2,0:T(8,128)(2,1)}, u32[]{:S(2)}) %copy-start.2) | copy-done | bytes 2359320
  41.7 2.0 %local_partial.4.a_ref = bf16[528,512]{1,0:T(8,128)(2,1)S(1)} custom-call(bf16[8,288,128]{2,1,0:T(8,128)(2,1)S(1)} %all-to-all-done.refs_0_, bf16[2,576,1024]{2,1,0:T(8,128)(2,1)S(1)} %bitcast.19, f32[2,8,1024]{2,1,0:T(8,128)S(1)} %select_bitcast_fusion.refs_2_), custom_call_target="tpu_custom_call" | custom-call | flops 1207959552 | bytes 4194304 | tf_op jit(solution)/shard_map/local_partial/pallas_call | solution.py:122
  43.7 5.2 %collective-permute-done.4.refs_0_ = bf16[8,288,128]{2,1,0:T(8,128)(2,1)S(1)} collective-permute-done((bf16[8,288,128]{2,1,0:T(8,128)(2,1)S(1)}, bf16[8,288,128]{2,1,0:T(8,128)(2,1)S(1)}, u32[]{:S(2)}, u32[]{:S(2)}) %collective-permute-start.4) | collective-permute-done | bytes 589856 | tf_op jit(solution)/shard_map/ppermute | solution.py:292
  49.0 2.0 %local_partial.7 = bf16[528,512]{1,0:T(8,128)(2,1)S(1)} custom-call(bf16[8,288,128]{2,1,0:T(8,128)(2,1)S(1)} %collective-permute-done.4.refs_0_, bf16[2,576,1024]{2,1,0:T(8,128)(2,1)S(1)} %bitcast.20, f32[2,8,1024]{2,1,0:T(8,128)S(1)} %select_bitcast_fusion.refs_2_), custom_call_target="tpu_custom_call" | custom-call | flops 1207959552 | bytes 4194304 | tf_op jit(solution)/shard_map/local_partial/pallas_call | solution.py:122
  50.9 5.0 %collective-permute-start.5 = (bf16[528,512]{1,0:T(8,128)(2,1)S(1)}, bf16[528,512]{1,0:T(8,128)(2,1)S(1)}, u32[]{:S(2)}, u32[]{:S(2)}) collective-permute-start(bf16[528,512]{1,0:T(8,128)(2,1)S(1)} %local_partial.7), channel_id=1, source_target_pairs={{0,256},{128,384},{256,0},{384,128},{1,257},{129,385},{257,1},{385... | collective-permute-start | bytes 1622024 | tf_op jit(solution)/shard_map/ppermute | solution.py:292
  55.9 5.8 %collective-permute-done.2.refs_0_ = bf16[8,288,128]{2,1,0:T(8,128)(2,1)S(1)} collective-permute-done((bf16[8,288,128]{2,1,0:T(8,128)(2,1)S(1)}, bf16[8,288,128]{2,1,0:T(8,128)(2,1)S(1)}, u32[]{:S(2)}, u32[]{:S(2)}) %collective-permute-start.2) | collective-permute-done | bytes 589856 | tf_op jit(solution)/shard_map/ppermute | solution.py:292
  61.7 2.0 %local_partial.6 = bf16[528,512]{1,0:T(8,128)(2,1)S(1)} custom-call(bf16[8,288,128]{2,1,0:T(8,128)(2,1)S(1)} %collective-permute-done.2.refs_0_, bf16[2,576,1024]{2,1,0:T(8,128)(2,1)S(1)} %bitcast.21, f32[2,8,1024]{2,1,0:T(8,128)S(1)} %select_bitcast_fusion.refs_2_), custom_call_target="tpu_custom_call" | custom-call | flops 1207959552 | bytes 4194304 | tf_op jit(solution)/shard_map/local_partial/pallas_call | solution.py:122
  63.7 3.2 %collective-permute-start.3 = (bf16[528,512]{1,0:T(8,128)(2,1)S(1)}, bf16[528,512]{1,0:T(8,128)(2,1)S(1)}, u32[]{:S(2)}, u32[]{:S(2)}) collective-permute-start(bf16[528,512]{1,0:T(8,128)(2,1)S(1)} %local_partial.6), channel_id=1, source_target_pairs={{0,128},{128,256},{256,384},{384,0},{1,129},{129,257},{257,385},{3... | collective-permute-start | bytes 1622024 | tf_op jit(solution)/shard_map/ppermute | solution.py:292
  66.9 2.0 %local_partial.5 = bf16[528,512]{1,0:T(8,128)(2,1)S(1)} custom-call(bf16[8,288,128]{2,1,0:T(8,128)(2,1)S(1)} %collective-permute-done.refs_0_, bf16[2,576,1024]{2,1,0:T(8,128)(2,1)S(1)} %bitcast.22, f32[2,8,1024]{2,1,0:T(8,128)S(1)} %select_bitcast_fusion.refs_2_), custom_call_target="tpu_custom_call" | custom-call | flops 1207959552 | bytes 4194304 | tf_op jit(solution)/shard_map/local_partial/pallas_call | solution.py:122
  68.9 4.0 %collective-permute-start.1 = (bf16[528,512]{1,0:T(8,128)(2,1)S(1)}, bf16[528,512]{1,0:T(8,128)(2,1)S(1)}, u32[]{:S(2)}, u32[]{:S(2)}) collective-permute-start(bf16[528,512]{1,0:T(8,128)(2,1)S(1)} %local_partial.5), channel_id=1, source_target_pairs={{0,384},{128,0},{256,128},{384,256},{1,385},{129,1},{257,129},{385... | collective-permute-start | bytes 1622024 | tf_op jit(solution)/shard_map/ppermute | solution.py:292
  72.9 7.9 %collective-permute-done.3.c_ref = bf16[528,512]{1,0:T(8,128)(2,1)S(1)} collective-permute-done((bf16[528,512]{1,0:T(8,128)(2,1)S(1)}, bf16[528,512]{1,0:T(8,128)(2,1)S(1)}, u32[]{:S(2)}, u32[]{:S(2)}) %collective-permute-start.3) | collective-permute-done | bytes 540704 | tf_op jit(solution)/shard_map/ppermute | solution.py:292
  80.8 3.9 %collective-permute-done.1.b_ref = bf16[528,512]{1,0:T(8,128)(2,1)S(1)} collective-permute-done((bf16[528,512]{1,0:T(8,128)(2,1)S(1)}, bf16[528,512]{1,0:T(8,128)(2,1)S(1)}, u32[]{:S(2)}, u32[]{:S(2)}) %collective-permute-start.1) | collective-permute-done | bytes 540704 | tf_op jit(solution)/shard_map/ppermute | solution.py:292
  84.7 1.4 combine_x.1
  86.1 5.0 %all-to-all-start.1 = ((bf16[8,272,128]{2,1,0:T(8,128)(2,1)}), bf16[8,272,128]{2,1,0:T(8,128)(2,1)S(1)}, u32[]{:S(2)}, u32[]{:S(2)}) async-start(bf16[8,272,128]{2,1,0:T(8,128)(2,1)} %combine_x.1), calls=%async_computation.1 | async-start | bytes 1114112 | tf_op jit(solution)/shard_map/all_to_all | solution.py:300
  91.2 1.6 %own_part.1 = (f32[64,512]{1,0:T(8,128)S(1)}, f32[64,128]{1,0:T(8,128)S(1)}) custom-call(bf16[8,288,128]{2,1,0:T(8,128)(2,1)} %pack_queries.1.q_ref, bf16[2,128,576]{2,1,0:T(8,128)(2,1)S(1)} %pad.4.fresh_ref, f32[8,128]{1,0:T(8,128)S(1)} %fusion.bias_ref), custom_call_target="tpu_custom_call" | custom-call | tf_op jit(solution)/shard_map/own_part/pallas_call | solution.py:206
  92.8 14.6 %all-to-all-done.1.got_ref = bf16[8,272,128]{2,1,0:T(8,128)(2,1)S(1)} async-done(((bf16[8,272,128]{2,1,0:T(8,128)(2,1)}), bf16[8,272,128]{2,1,0:T(8,128)(2,1)S(1)}, u32[]{:S(2)}, u32[]{:S(2)}) %all-to-all-start.1) | async-done | bytes 557088 | tf_op jit(solution)/shard_map/all_to_all | solution.py:300
  107.5 0.7 merge_up.1
  108.2 18.2 %all_to_all.20 = bf16[16,16,512]{2,1,0:T(8,128)(2,1)S(1)} all-to-all(bf16[16,16,512]{2,1,0:T(8,128)(2,1)S(1)} %merge_up.1), channel_id=1, replica_groups=mesh['x'=4,'z'=8,'y'=8,'core'=2] {'y','core'}, dimensions={0} | all-to-all | bytes 524288 | tf_op jit(solution)/shard_map/all_to_all | solution.py:300
  126.4 0.4 project_out.1
  126.8 19.0 %all_to_all.21 = bf16[32,8,448]{2,1,0:T(8,128)(2,1)S(1)} all-to-all(bf16[32,8,448]{2,1,0:T(8,128)(2,1)S(1)} %bitcast.16), channel_id=1, replica_groups=mesh['x'=4,'z'=8,'y'=8,'core'=2] {'x','z'}, dimensions={0} | all-to-all | bytes 458752 | tf_op jit(solution)/shard_map/all_to_all | solution.py:300
  145.8 0.7 reduce_sum.12
  (16 shorter events, 0.1 us)
Async XLA Ops:
  1.9 27.4 %all-to-all-start = ((bf16[8,288,128]{2,1,0:T(8,128)(2,1)}), bf16[8,288,128]{2,1,0:T(8,128)(2,1)S(1)}, u32[]{:S(2)}, u32[]{:S(2)}) async-start(bf16[8,288,128]{2,1,0:T(8,128)(2,1)} %pack_queries.1.q_ref), calls=%async_computation | async-start | bytes 1179648 | tf_op jit(solution)/shard_map/all_to_all | solution.py:300
  29.3 19.7 %collective-permute-start.4 = (bf16[8,288,128]{2,1,0:T(8,128)(2,1)S(1)}, bf16[8,288,128]{2,1,0:T(8,128)(2,1)S(1)}, u32[]{:S(2)}, u32[]{:S(2)}) collective-permute-start(bf16[8,288,128]{2,1,0:T(8,128)(2,1)S(1)} %all-to-all-done.refs_0_), channel_id=1, source_target_pairs={{0,256},{128,384},{256,0},{384,128},{1,257},{129,385},{257,1},{385... | collective-permute-start | bytes 1769480 | tf_op jit(solution)/shard_map/ppermute | solution.py:292
  34.2 27.5 %collective-permute-start.2 = (bf16[8,288,128]{2,1,0:T(8,128)(2,1)S(1)}, bf16[8,288,128]{2,1,0:T(8,128)(2,1)S(1)}, u32[]{:S(2)}, u32[]{:S(2)}) collective-permute-start(bf16[8,288,128]{2,1,0:T(8,128)(2,1)S(1)} %all-to-all-done.refs_0_), channel_id=1, source_target_pairs={{0,384},{128,0},{256,128},{384,256},{1,385},{129,1},{257,129},{385... | collective-permute-start | bytes 1769480 | tf_op jit(solution)/shard_map/ppermute | solution.py:292
  37.3 29.6 %collective-permute-start = (bf16[8,288,128]{2,1,0:T(8,128)(2,1)S(1)}, bf16[8,288,128]{2,1,0:T(8,128)(2,1)S(1)}, u32[]{:S(2)}, u32[]{:S(2)}) collective-permute-start(bf16[8,288,128]{2,1,0:T(8,128)(2,1)S(1)} %all-to-all-done.refs_0_), channel_id=1, source_target_pairs={{0,128},{128,256},{256,384},{384,0},{1,129},{129,257},{257,385},{3... | collective-permute-start | bytes 1769480 | tf_op jit(solution)/shard_map/ppermute | solution.py:292
  40.1 1.7 %copy-start.2 = (bf16[2,1024,576]{1,2,0:T(8,128)(2,1)S(1)}, bf16[2,1024,576]{1,2,0:T(8,128)(2,1)}, u32[]{:S(2)}) copy-start(bf16[2,1024,576]{1,2,0:T(8,128)(2,1)} %param.7) | copy-start | bytes 7077892
  50.9 22.0 %collective-permute-start.5 = (bf16[528,512]{1,0:T(8,128)(2,1)S(1)}, bf16[528,512]{1,0:T(8,128)(2,1)S(1)}, u32[]{:S(2)}, u32[]{:S(2)}) collective-permute-start(bf16[528,512]{1,0:T(8,128)(2,1)S(1)} %local_partial.7), channel_id=1, source_target_pairs={{0,256},{128,384},{256,0},{384,128},{1,257},{129,385},{257,1},{385... | collective-permute-start | bytes 1622024 | tf_op jit(solution)/shard_map/ppermute | solution.py:292
  63.7 17.1 %collective-permute-start.3 = (bf16[528,512]{1,0:T(8,128)(2,1)S(1)}, bf16[528,512]{1,0:T(8,128)(2,1)S(1)}, u32[]{:S(2)}, u32[]{:S(2)}) collective-permute-start(bf16[528,512]{1,0:T(8,128)(2,1)S(1)} %local_partial.6), channel_id=1, source_target_pairs={{0,128},{128,256},{256,384},{384,0},{1,129},{129,257},{257,385},{3... | collective-permute-start | bytes 1622024 | tf_op jit(solution)/shard_map/ppermute | solution.py:292
  68.9 22.2 %copy-start.3 = (bf16[8,2,576]{2,1,0:T(2,128)(2,1)S(1)}, bf16[8,2,576]{2,1,0:T(2,128)(2,1)}, u32[]{:S(2)}) copy-start(bf16[8,2,576]{2,1,0:T(2,128)(2,1)} %param.9) | copy-start | bytes 55300
  68.9 38.6 %copy-start = (bf16[4,512,128]{2,1,0:T(8,128)(2,1)S(1)}, bf16[4,512,128]{2,1,0:T(8,128)(2,1)}, u32[]{:S(2)}) copy-start(bf16[4,512,128]{2,1,0:T(8,128)(2,1)} %up_ref.1) | copy-start | bytes 1572868
  68.9 15.8 %collective-permute-start.1 = (bf16[528,512]{1,0:T(8,128)(2,1)S(1)}, bf16[528,512]{1,0:T(8,128)(2,1)S(1)}, u32[]{:S(2)}, u32[]{:S(2)}) collective-permute-start(bf16[528,512]{1,0:T(8,128)(2,1)S(1)} %local_partial.5), channel_id=1, source_target_pairs={{0,384},{128,0},{256,128},{384,256},{1,385},{129,1},{257,129},{385... | collective-permute-start | bytes 1622024 | tf_op jit(solution)/shard_map/ppermute | solution.py:292
  86.1 40.3 %copy-start.1 = (bf16[512,448]{0,1:T(8,128)(2,1)S(1)}, bf16[512,448]{0,1:T(8,128)(2,1)}, u32[]{:S(2)}) copy-start(bf16[512,448]{0,1:T(8,128)(2,1)} %param.13) | copy-start | bytes 1376260
  86.1 21.3 %all-to-all-start.1 = ((bf16[8,272,128]{2,1,0:T(8,128)(2,1)}), bf16[8,272,128]{2,1,0:T(8,128)(2,1)S(1)}, u32[]{:S(2)}, u32[]{:S(2)}) async-start(bf16[8,272,128]{2,1,0:T(8,128)(2,1)} %combine_x.1), calls=%async_computation.1 | async-start | bytes 1114112 | tf_op jit(solution)/shard_map/all_to_all | solution.py:300
